TPU v7x, 32 devices: a whole 2x2x4 slice. The times are simulated.
32 devices in a mesh: gz: 4 (over z), gy: 4 (over x, core), gx: 2 (over y).
Axes of the slice: x: 2, y: 2, z: 4, core: 2. Of those that a mesh axis runs over, the one named last changes fastest.
Arguments:
- stacks: bfloat16 [32, 32, 512], P('gz', 'gy', 'gx'), may hold values from -6 to 6
- offsets: int32 [2], replicated, may hold values from -32 to 32, as said below
- ramp_width: int32 [2], replicated, may hold values from 17 to 64, as said below
- stem_weight: bfloat16 [27, 32], replicated, may hold values from -1.25 to 1.25
- stem_bias: float32 [32], replicated, may hold values from -3 to 3
- layer_weight: bfloat16 [4, 27, 32, 32], replicated, may hold values from -0.21875 to 0.21875
- layer_bias: float32 [4, 32], replicated, may hold values from -3 to 3
- head_weight: bfloat16 [32], replicated, may hold values from -1 to 1
Outputs:
- logits: float32 [32, 32, 256], P('gz', 'gy', 'gx')
Inputs may be any that keep to these rules, and one draw needn't show every extreme that they name: `offsets`: each tile stack's shift; in every draw some stack is shifted by 32. `ramp_width`: each tile stack's ramp width; in every draw some stack has width 64 // 4 + 1 and another width 64.
All inputs are finite; a program needn't handle non-finite values.
Results may differ from a plain program's by a relative error of at most 0.0096.
Values may be sent and summed in bfloat16 or wider, within the bound.
No kernel may reach another device: no remote copies, remote signals or barrier semaphores. Data moves between devices by JAX's collectives and lax.ppermute only.
A program may use at most 128 MiB of HBM per device.

v0:
```python
import jax
import jax.numpy as jnp
from jax import lax
from jax.experimental import pallas as pl
from jax.experimental.pallas import tpu as pltpu
from jax.sharding import PartitionSpec as P

LAYERS = 4
H = 64
S = 32
BX = 128
C = 32
REACH = 16
SLAB = 8
WIDE = SLAB + 2 * REACH
NZ = 32
NY = 32
GROUPS = (10, 9, 8, 6, 2)
TAPS = (2, 2, 3, 3)
STEP = (1, 1, 1, 2)
ORIGIN = (-15, -14, -12, -8, 0)
BF = jnp.bfloat16
F32 = jnp.float32


def blend_weight(position, width, tile_len):
    spot = position.astype(F32)
    return jnp.minimum(1.0, jnp.minimum((spot + 1.0) / width, (tile_len - spot) / width))


def table_entry(table, wanted):
    slots = jnp.arange(table.shape[0])
    return jnp.sum(jnp.where(slots == wanted, table, 0))


def weights_kernel(lw_ref, sw_ref, ws_ref, *w_refs):
    lane = lax.broadcasted_iota(jnp.int32, (C, 4 * C), 1) // C
    zero = jnp.zeros((C, 4 * C), BF)
    for layer in range(LAYERS):
        spacing = 2**layer
        out = w_refs[layer]

        def per_row_tap(s, carry, layer=layer, spacing=spacing, out=out):
            taps = [
                [lw_ref[layer, 9 * c + a + 3 * s].astype(F32) for a in range(3)] for c in range(3)
            ]
            for i in range(TAPS[layer]):
                for xi in range(4):
                    rows = pl.ds(xi * C, C)
                    for c in range(3):
                        block = jnp.zeros((C, 4 * C), F32)
                        for a in range(3):
                            xo = 4 * STEP[layer] * i + xi - spacing * a
                            if 0 <= xo < 4:
                                block = jnp.where(lane == xo, taps[c][a], block)
                        block = block.astype(BF)
                        out[s, i, c, rows, 0 : 4 * C] = block
                        out[s, i, c + 1, rows, 4 * C : 8 * C] = block
                    out[s, i, 0, rows, 4 * C : 8 * C] = zero
                    out[s, i, 3, rows, 0 : 4 * C] = zero
            return carry

        lax.fori_loop(0, 3, per_row_tap, 0)
    row = lax.broadcasted_iota(jnp.int32, (128, 8 * C), 0)
    column = lax.broadcasted_iota(jnp.int32, (128, 8 * C), 1) // C

    def per_tile(k, carry):
        diff = row - column - 8 * k
        for c in range(3):
            block = jnp.zeros((128, 8 * C), F32)
            for b in range(3):
                for a in range(3):
                    tap = 9 * c + 3 * b + a
                    block = jnp.where(diff == WIDE * b + a, sw_ref[tap : tap + 1, :], block)
            ws_ref[k, 128 * c : 128 * (c + 1), :] = block.astype(BF)
        return carry

    lax.fori_loop(0, GROUPS[0] // 2, per_tile, 0)


def shifted(value, by):
    rows = value.shape[0]
    spot = lax.broadcasted_iota(jnp.int32, value.shape, 0) % NY
    moved = pltpu.roll(value, by % rows, 0)
    keep = (spot >= by) if by > 0 else (spot < NY + by)
    return jnp.where(keep, moved, 0.0)


def conv_kernel(
    cols_ref, image_ref, ws_ref, w0, w1, w2, w3, sb_ref, lb_ref, head_ref, out_ref, stem_in, *acts
):
    w_refs = (w0, w1, w2, w3)
    first_col = cols_ref[0]
    total_cols = cols_ref[1]

    def col_mask(layer, group, width):
        lane = lax.broadcasted_iota(jnp.int32, (1, width * C), 1) // C
        col = lane + (4 * group + first_col + ORIGIN[layer])
        return jnp.where((col >= 0) & (col < total_cols), 1.0, 0.0)

    for layer in range(LAYERS):
        spacing = 2**layer
        pad = jnp.zeros((3, spacing, NY, 4 * C), BF)
        for g in range(GROUPS[layer]):
            acts[layer][:, g, 1, :, 0] = pad
            acts[layer][:, g, 0, :, NZ // (2 * spacing) + 1] = pad

    image = image_ref[...].astype(F32).reshape(NZ * NY, WIDE)
    stem_in[...] = jnp.zeros(stem_in.shape, BF)
    blank = jnp.zeros((NZ * NY, 128 - 3 * WIDE), F32)
    packed = jnp.concatenate([shifted(image, 1), image, shifted(image, -1), blank], axis=1)
    stem_in[1 : NZ + 1] = packed.astype(BF).reshape(NZ, NY, 128)

    def store(layer, group, plane_sets):
        spacing = 2**layer
        for lead, value in plane_sets:
            for s in range(3):
                part = value if s == 1 else shifted(value, spacing if s == 0 else -spacing)
                planes = part.astype(BF).reshape(lead[1], NZ // (2 * spacing), 2, NY, 4 * C)
                for b in range(2):
                    acts[layer][
                        s, group, b, lead[0] : lead[0] + lead[1], 1 : 1 + NZ // (2 * spacing)
                    ] = planes[:, :, b]

    def stem_tile(k, carry):
        lhs = jnp.concatenate(
            [stem_in[c : c + NZ].reshape(NZ * NY, 128) for c in range(3)], axis=1
        )
        acc = jnp.dot(lhs, ws_ref[k], preferred_element_type=F32)
        acc = jnp.maximum(acc + sb_ref[...], 0.0) * col_mask(0, 2 * k, 8)
        store(0, 2 * k, [((0, 1), acc[:, : 4 * C])])
        store(0, 2 * k + 1, [((0, 1), acc[:, 4 * C :])])
        return carry

    lax.fori_loop(0, GROUPS[0] // 2, stem_tile, 0)

    for layer in range(LAYERS):
        spacing = 2**layer
        count = NZ // (2 * spacing)
        src = acts[layer]

        def conv_group(g, carry, layer=layer, spacing=spacing, count=count, src=src):
            pieces = []
            for s in range(3):
                for i in range(TAPS[layer]):
                    for t in range(4):
                        piece = src[
                            s,
                            g + STEP[layer] * i,
                            1 - t % 2,
                            :,
                            (t + 1) // 2 : (t + 1) // 2 + count,
                        ]
                        pieces.append(piece.reshape(NZ * NY // 2, 4 * C))
            lhs = jnp.concatenate(pieces, axis=1)
            weights = w_refs[layer][...].reshape(3 * TAPS[layer] * 4 * 128, 8 * C)
            acc = jnp.dot(lhs, weights, preferred_element_type=F32)
            mask = col_mask(layer + 1, g, 4)
            halves = []
            for b in range(2):
                if layer < 2:
                    pair = jnp.concatenate(
                        [
                            src[1, g + i, b, :, 1 : 1 + count].reshape(NZ * NY // 2, 4 * C)
                            for i in range(2)
                        ],
                        axis=1,
                    ).astype(F32)
                    centre = pair[:, spacing * C : spacing * C + 4 * C]
                else:
                    centre = src[1, g + STEP[layer], b, :, 1 : 1 + count]
                    centre = centre.reshape(NZ * NY // 2, 4 * C).astype(F32)
                half = acc[:, 4 * C * b : 4 * C * (b + 1)] + lb_ref[layer]
                halves.append(centre + jnp.maximum(half, 0.0) * mask)
            if layer + 1 < LAYERS:
                store(layer + 1, g, [((spacing * b, spacing), halves[b]) for b in range(2)])
            else:
                last = jnp.concatenate(halves, axis=1).astype(BF)
                out_ref[g] = lax.dot_general(
                    head_ref[...], last, (((1,), (1,)), ((), ())), preferred_element_type=F32
                )
            return carry

        lax.fori_loop(0, GROUPS[layer + 1], conv_group, 0)


def vmem():
    return pl.BlockSpec(memory_space=pltpu.VMEM)


def body(
    stacks, offsets, ramp_width, stem_weight, stem_bias, layer_weight, layer_bias, head_weight
):
    depth_b, rows_b, tile_len = stacks.shape
    depth_parts, row_parts = lax.axis_size("gz"), lax.axis_size("gy")
    parts = depth_parts * row_parts
    column_idx = lax.axis_index("gx")
    column_cnt = lax.axis_size("gx")
    slab_idx = lax.axis_index("gz") * row_parts + lax.axis_index("gy")
    assert (depth_b * depth_parts, rows_b * row_parts, parts * SLAB) == (NZ, NY, BX)

    edge = H + S + REACH
    low_end = stacks[:, :, tile_len - edge :]
    high_end = stacks[:, :, :edge]
    if column_cnt == 2:
        got = lax.ppermute(jnp.where(column_idx == 0, low_end, high_end), "gx", [(0, 1), (1, 0)])
        from_lower, from_upper = got, got
    else:
        forward = [(i, i + 1) for i in range(column_cnt - 1)]
        from_lower = lax.ppermute(low_end, "gx", forward)
        from_upper = lax.ppermute(high_end, "gx", [(b, a) for a, b in forward])

    tiled = jnp.tile(jnp.swapaxes(layer_weight, 2, 3), (1, 1, 1, 4))
    stem_tiled = jnp.tile(stem_weight.astype(F32), (1, 8))
    shapes = [jax.ShapeDtypeStruct((GROUPS[0] // 2, 384, 8 * C), BF)] + [
        jax.ShapeDtypeStruct((3, TAPS[layer], 4, 4 * C, 8 * C), BF) for layer in range(LAYERS)
    ]
    weights = pl.pallas_call(
        weights_kernel,
        out_shape=shapes,
        in_specs=[vmem(), vmem()],
        out_specs=[vmem()] * 5,
        compiler_params=pltpu.CompilerParams(vmem_limit_bytes=40 * 2**20),
        cost_estimate=pl.CostEstimate(flops=4000000, bytes_accessed=9000000, transcendentals=0),
    )(tiled, stem_tiled)

    shift_own = table_entry(offsets, column_idx)
    shift_lower = table_entry(offsets, column_idx - 1)
    shift_upper = table_entry(offsets, column_idx + 1)
    ramp_own = table_entry(ramp_width, column_idx).astype(F32)
    ramp_lower = table_entry(ramp_width, column_idx - 1).astype(F32)
    ramp_upper = table_entry(ramp_width, column_idx + 1).astype(F32)
    ramp_lower = jnp.where(column_idx > 0, ramp_lower, 1.0)
    ramp_upper = jnp.where(column_idx < column_cnt - 1, ramp_upper, 1.0)
    span = BX + 2 * REACH
    columns = jnp.arange(span) - REACH
    filler = jnp.zeros((depth_b, rows_b, span), BF)
    own_vals = lax.dynamic_slice_in_dim(stacks, H - REACH - shift_own, span, 2).astype(F32)
    lower_vals = lax.dynamic_slice_in_dim(
        jnp.concatenate([from_lower, filler], 2), S - shift_lower, span, 2
    ).astype(F32)
    upper_vals = lax.dynamic_slice_in_dim(
        jnp.concatenate([filler, from_upper], 2), H + REACH - shift_upper, span, 2
    ).astype(F32)
    weight_own = blend_weight(columns + H - shift_own, ramp_own, tile_len)
    lower_pos = columns + BX + H - shift_lower
    weight_lower = jnp.where(
        (lower_pos < tile_len) & (column_idx > 0),
        blend_weight(lower_pos, ramp_lower, tile_len),
        0.0,
    )
    upper_pos = columns - BX + H - shift_upper
    weight_upper = jnp.where(
        (upper_pos >= 0) & (column_idx < column_cnt - 1),
        blend_weight(upper_pos, ramp_upper, tile_len),
        0.0,
    )
    numerator = own_vals * weight_own + lower_vals * weight_lower + upper_vals * weight_upper
    blended = numerator / (weight_own + weight_lower + weight_upper)
    global_col = columns + column_idx * BX
    blended = jnp.where((global_col >= 0) & (global_col < column_cnt * BX), blended, 0.0)
    blended = blended.astype(BF)
    slabs = jnp.stack([blended[:, :, SLAB * j : SLAB * j + WIDE] for j in range(parts)])
    slabs = lax.all_to_all(slabs, ("gz", "gy"), 0, 0, tiled=True)
    image = slabs.reshape(depth_parts, row_parts, depth_b, rows_b, WIDE)
    image = image.transpose(0, 2, 1, 3, 4).reshape(NZ, NY, WIDE)

    cols = jnp.stack([column_idx * BX + slab_idx * SLAB, column_cnt * BX]).astype(jnp.int32)
    stem_bias_row = jnp.tile(stem_bias[None], (1, 8))
    bias_rows = jnp.tile(layer_bias[:, None], (1, 1, 4))
    head_rows = jnp.kron(jnp.eye(8, dtype=F32), head_weight.astype(F32)[None]).astype(BF)
    scratch = [pltpu.VMEM((NZ + 2, NY, 128), BF)] + [
        pltpu.VMEM((3, GROUPS[layer], 2, 2**layer, NZ // 2 ** (layer + 1) + 2, NY, 4 * C), BF)
        for layer in range(LAYERS)
    ]
    flat = pl.pallas_call(
        conv_kernel,
        out_shape=jax.ShapeDtypeStruct((2, 8, NZ * NY // 2), F32),
        in_specs=[pl.BlockSpec(memory_space=pltpu.SMEM)] + [vmem()] * 9,
        out_specs=vmem(),
        scratch_shapes=scratch,
        compiler_params=pltpu.CompilerParams(vmem_limit_bytes=60 * 2**20),
        cost_estimate=pl.CostEstimate(
            flops=20000000000, bytes_accessed=9000000, transcendentals=0
        ),
    )(cols, image, *weights, stem_bias_row, bias_rows, head_rows)

    pieces = flat.reshape(2, 2, 4, 8, 2, row_parts, rows_b).transpose(4, 1, 5, 0, 2, 3, 6)
    pieces = pieces.reshape(parts, SLAB, depth_b * rows_b)
    pieces = lax.all_to_all(pieces, ("gz", "gy"), 0, 0, tiled=True)
    return pieces.reshape(BX, depth_b * rows_b).T.reshape(depth_b, rows_b, BX)


def solution(mesh):
    return jax.shard_map(
        body,
        mesh=mesh,
        in_specs=(P("gz", "gy", "gx"), P(), P(), P(), P(), P(), P(), P()),
        out_specs=P("gz", "gy", "gx"),
        check_vma=False,
    )
```

profile of v0, /device:TPU:0, one launch (start us, length us, event | category | flops | bytes accessed | tf_op | source)
XLA Modules:
  0.0 103.7 jit_solution(3300513504627653758)
XLA Ops:
  0.0 0.8 slice_select_fusion
  0.8 3.0 %collective-permute-start = (bf16[8,8,112]{2,1,0:T(8,128)(2,1)S(1)}, bf16[8,8,112]{2,1,0:T(8,128)(2,1)S(1)}, u32[]{:S(2)}, u32[]{:S(2)}) collective-permute-start(bf16[8,8,112]{2,1,0:T(8,128)(2,1)S(1)} %slice_select_fusion), channel_id=1, source_target_pairs={{0,1},{1,0},{2,3},{3,2},{4,5},{5,4},{6,7},{7,6},{8,9},{9,8},{10,11... | collective-permute-start | bytes 43016 | tf_op jit(solution)/shard_map/ppermute | solution.py:206
  3.8 1.4 %fusion.2 = (s32[]{:T(128)}, s32[]{:T(128)}, s32[]{:T(128)}, s32[]{:T(128)}, s32[]{:T(128)}, /*index=5*/s32[]{:T(128)}) fusion(s32[2]{0:T(128)} %param.9, s32[]{:T(128)S(6)} %axis_index.32, s32[]{:T(128)S(6)} %add.156, s32[]{:T(128)S(6)} %sub.92, s32[2]{0:T(128)} %param.10), kind=kLoop, calls=%fused_computation.54 | loop fusion | flops 24 | bytes 52 | tf_op jit(solution)/shard_map/reduce_sum | solution.py:33
  7.1 0.7 fusion.1
  7.8 1.9 %add_add_fusion = (f32[160]{0:T(256)S(1)}, f32[160]{0:T(256)S(1)}, f32[160]{0:T(256)S(1)}) fusion(f32[]{:T(128)S(6)} %convert_element_type.69, s32[]{:T(128)} %get-tuple-element.15, f32[]{:T(128)S(6)} %select_n.76, pred[]{:T(512)S(6)} %gt.4, s32[]{:T(128)} %get-tuple-element.17, f32[]{:T(128)S(6)} %select_n.81, pred[]{:T(512)S(6)} %lt.31, s32[]{:T(128)} %get-tuple-element.16), kind=kLoop, calls=%fused_computation.52 | loop fusion | flops 5600 | bytes 1946 | tf_op jit(solution)/shard_map/add | solution.py:259
  13.7 0.7 mul.74
  14.4 0.9 select_convert_fusion
  16.5 1.0 reshape.110
  17.6 5.9 %all-to-all-start = ((bf16[16,2,1280]{2,1,0:T(2,128)(2,1)}), bf16[16,2,1280]{2,1,0:T(2,128)(2,1)S(1)}, u32[]{:S(2)}, u32[]{:S(2)}) async-start(bf16[16,2,1280]{2,1,0:T(2,128)(2,1)} %reshape.110), calls=%async_computation | async-start | bytes 163840 | tf_op jit(solution)/shard_map/all_to_all | solution.py:264
  23.5 0.6 multiply_convert_fusion.head_ref
  24.1 1.5 %copy.16 = bf16[4,27,32,32]{3,2,1,0:T(8,128)(2,1)S(1)} copy(bf16[4,27,32,32]{2,3,1,0:T(8,128)(2,1)} %bitcast.81) | data formatting | bytes 442368 | tf_op jit(solution)/shard_map/transpose | solution.py:213
  25.6 3.8 %tile.16 = bf16[4,27,32,4,32]{4,3,2,1,0:T(4,128)(2,1)} broadcast(bf16[4,27,32,32]{3,2,1,0:T(8,128)(2,1)S(1)} %copy.16), dimensions={0,1,2,4} | broadcast | bytes 1105920 | tf_op jit(solution)/shard_map/tile | solution.py:213
  29.4 4.6 %tile.17.lw_ref = bf16[4,27,32,128]{3,2,1,0:T(8,128)(2,1)S(1)} reshape(bf16[4,27,32,4,32]{4,3,2,1,0:T(4,128)(2,1)} %tile.16) | data formatting | bytes 1769472 | tf_op jit(solution)/shard_map/tile | solution.py:213
  34.1 0.7 tile.41.lb_ref
  34.8 0.6 tile.39.sb_ref
  35.4 2.3 %shard_map.82 = (bf16[5,384,256]{2,1,0:T(8,128)(2,1)S(1)}, bf16[3,2,4,128,256]{4,3,2,1,0:T(8,128)(2,1)S(1)}, bf16[3,2,4,128,256]{4,3,2,1,0:T(8,128)(2,1)S(1)}, b...) custom-call(bf16[4,27,32,128]{3,2,1,0:T(8,128)(2,1)S(1)} %tile.17.lw_ref, f32[27,256]{1,0:T(8,128)S(1)} %tile.37.sw_ref), custom_call_target="tpu_custom_call" | custom-call | flops 4000000 | bytes 9000000 | tf_op jit(solution)/shard_map/pallas_call | solution.py:218
  37.7 1.4 %copy-done = bf16[3,3,4,128,256]{4,3,2,1,0:T(8,128)(2,1)} copy-done((bf16[3,3,4,128,256]{4,3,2,1,0:T(8,128)(2,1)}, bf16[3,3,4,128,256]{4,3,2,1,0:T(8,128)(2,1)S(1)}, u32[]{:S(2)}) %copy-start) | copy-done | bytes 2359320
  39.1 1.4 %copy-done.1 = bf16[3,3,4,128,256]{4,3,2,1,0:T(8,128)(2,1)} copy-done((bf16[3,3,4,128,256]{4,3,2,1,0:T(8,128)(2,1)}, bf16[3,3,4,128,256]{4,3,2,1,0:T(8,128)(2,1)S(1)}, u32[]{:S(2)}) %copy-start.1) | copy-done | bytes 2359320
  40.5 1.2 %copy-done.2 = bf16[3,2,4,128,256]{4,3,2,1,0:T(8,128)(2,1)} copy-done((bf16[3,2,4,128,256]{4,3,2,1,0:T(8,128)(2,1)}, bf16[3,2,4,128,256]{4,3,2,1,0:T(8,128)(2,1)S(1)}, u32[]{:S(2)}) %copy-start.2) | copy-done | bytes 1572888
  41.7 1.1 %copy-done.3 = bf16[3,2,4,128,256]{4,3,2,1,0:T(8,128)(2,1)} copy-done((bf16[3,2,4,128,256]{4,3,2,1,0:T(8,128)(2,1)}, bf16[3,2,4,128,256]{4,3,2,1,0:T(8,128)(2,1)S(1)}, u32[]{:S(2)}) %copy-start.3) | copy-done | bytes 1572888
  42.8 1.1 %copy-done.4 = bf16[5,384,256]{2,1,0:T(8,128)(2,1)} copy-done((bf16[5,384,256]{2,1,0:T(8,128)(2,1)}, bf16[5,384,256]{2,1,0:T(8,128)(2,1)S(1)}, u32[]{:S(2)}) %copy-start.4) | copy-done | bytes 983064
  43.9 0.6 pad_add_fusion.cols_ref
  44.5 0.4 reshape.111
  44.9 0.8 copy.15
  45.6 41.8 %shard_map.83 = f32[2,8,512]{2,1,0:T(8,128)} custom-call(s32[2]{0:T(128)} %pad_add_fusion.cols_ref, bf16[32,32,40]{2,1,0:T(8,128)(2,1)} %bitcast.83, bf16[5,384,256]{2,1,0:T(8,128)(2,1)} %copy-done.4, bf16[3,2,4,128,256]{4,3,2,1,0:T(8,128)(2,1)} %copy-done.2, bf16[3,2,4,128,256]{4,3,2,1,0:T(8,128)(2,1)} %copy-done.3, bf16[3,3,4,128,256]{4,3,2,1,0:T(8,128)(2,1)} %copy-done, ...), custom_call_target="tpu_custom_call" | custom-call | flops 20000000000 | bytes 9000000 | tf_op jit(solution)/shard_map/pallas_call | solution.py:276
  87.4 1.4 %reshape.106 = f32[2,2,4,8,2,4,8]{6,5,4,3,2,1,0:T(4,128)S(1)} reshape(f32[2,8,512]{2,1,0:T(8,128)} %shard_map.83) | data formatting | bytes 65536 | tf_op jit(solution)/shard_map/reshape | solution.py:288
  88.8 0.1 copy.20
  88.9 0.2 reshape.107
  89.2 12.4 %all_to_all.10 = f32[16,1,512]{2,1,0:T(1,128)S(1)} all-to-all(f32[16,1,512]{2,1,0:T(1,128)S(1)} %reshape.112), channel_id=1, replica_groups=mesh['gz'=4,'gy'=4,'gx'=2] {'gz','gy'}, dimensions={0} | all-to-all | bytes 65536 | tf_op jit(solution)/shard_map/all_to_all | solution.py:290
  101.7 0.5 broadcast.278
  102.2 0.7 reduce
  103.0 0.7 copy.18
  (40 shorter events, 1.8 us)
Async XLA Ops:
  0.8 13.6 %collective-permute-start = (bf16[8,8,112]{2,1,0:T(8,128)(2,1)S(1)}, bf16[8,8,112]{2,1,0:T(8,128)(2,1)S(1)}, u32[]{:S(2)}, u32[]{:S(2)}) collective-permute-start(bf16[8,8,112]{2,1,0:T(8,128)(2,1)S(1)} %slice_select_fusion), channel_id=1, source_target_pairs={{0,1},{1,0},{2,3},{3,2},{4,5},{5,4},{6,7},{7,6},{8,9},{9,8},{10,11... | collective-permute-start | bytes 43016 | tf_op jit(solution)/shard_map/ppermute | solution.py:206
  17.6 26.9 %all-to-all-start = ((bf16[16,2,1280]{2,1,0:T(2,128)(2,1)}), bf16[16,2,1280]{2,1,0:T(2,128)(2,1)S(1)}, u32[]{:S(2)}, u32[]{:S(2)}) async-start(bf16[16,2,1280]{2,1,0:T(2,128)(2,1)} %reshape.110), calls=%async_computation | async-start | bytes 163840 | tf_op jit(solution)/shard_map/all_to_all | solution.py:264
  29.3 4.6 %copy-start.5 = (bf16[27,32]{1,0:T(8,128)(2,1)S(1)}, bf16[27,32]{1,0:T(8,128)(2,1)}, u32[]{:S(2)}) copy-start(bf16[27,32]{1,0:T(8,128)(2,1)} %param.11) | copy-start | bytes 5188
  29.4 4.8 %copy-start.6 = (f32[4,32]{1,0:T(4,128)S(1)}, f32[4,32]{1,0:T(4,128)}, u32[]{:S(2)}) copy-start(f32[4,32]{1,0:T(4,128)} %param.14) | copy-start | bytes 1540
  29.4 5.5 %copy-start.7 = (f32[32]{0:T(128)S(1)}, f32[32]{0:T(128)}, u32[]{:S(2)}) copy-start(f32[32]{0:T(128)} %param.12) | copy-start | bytes 388
  37.7 1.4 %copy-start = (bf16[3,3,4,128,256]{4,3,2,1,0:T(8,128)(2,1)}, bf16[3,3,4,128,256]{4,3,2,1,0:T(8,128)(2,1)S(1)}, u32[]{:S(2)}) copy-start(bf16[3,3,4,128,256]{4,3,2,1,0:T(8,128)(2,1)S(1)} %get-tuple-element.13.w2) | copy-start | bytes 7077892
  39.1 1.4 %copy-start.1 = (bf16[3,3,4,128,256]{4,3,2,1,0:T(8,128)(2,1)}, bf16[3,3,4,128,256]{4,3,2,1,0:T(8,128)(2,1)S(1)}, u32[]{:S(2)}) copy-start(bf16[3,3,4,128,256]{4,3,2,1,0:T(8,128)(2,1)S(1)} %get-tuple-element.14.w3) | copy-start | bytes 7077892
  40.5 1.2 %copy-start.2 = (bf16[3,2,4,128,256]{4,3,2,1,0:T(8,128)(2,1)}, bf16[3,2,4,128,256]{4,3,2,1,0:T(8,128)(2,1)S(1)}, u32[]{:S(2)}) copy-start(bf16[3,2,4,128,256]{4,3,2,1,0:T(8,128)(2,1)S(1)} %get-tuple-element.11.w0) | copy-start | bytes 4718596
  41.7 1.1 %copy-start.3 = (bf16[3,2,4,128,256]{4,3,2,1,0:T(8,128)(2,1)}, bf16[3,2,4,128,256]{4,3,2,1,0:T(8,128)(2,1)S(1)}, u32[]{:S(2)}) copy-start(bf16[3,2,4,128,256]{4,3,2,1,0:T(8,128)(2,1)S(1)} %get-tuple-element.12.w1) | copy-start | bytes 4718596
  42.8 1.1 %copy-start.4 = (bf16[5,384,256]{2,1,0:T(8,128)(2,1)}, bf16[5,384,256]{2,1,0:T(8,128)(2,1)S(1)}, u32[]{:S(2)}) copy-start(bf16[5,384,256]{2,1,0:T(8,128)(2,1)S(1)} %get-tuple-element.10.ws_ref) | copy-start | bytes 2949124
where the time goes:
time: 104 us
  Pallas kernels  44 us (42%)
  local copies, waits for them, and re-layouts  24.9 us (24%)
  blocking collectives  12.4 us (12%)
  starting transfers between devices  8.88 us (9%)
  other arithmetic  7.59 us (7%)
  between operations  5.86 us (6%)
    pallas_call x1, Pallas kernels, body(): pl.pallas_call(conv_kernel, out_shape=jax.ShapeDtypeStruct((2, 8, NZ * NY...  41.8 us
    all_to_all x1, blocking collectives, body(): pieces = lax.all_to_all(pieces, ('gz', 'gy'), 0, 0, tiled=True)  12.4 us
    unnamed x35, local copies, waits for them, and re-layouts  8.93 us
    another operation x2, local copies, waits for them, and re-layouts, body(): tiled = jnp.tile(jnp.swapaxes(layer_weight, 2, 3), (1, 1, 1, 4))  8.42 us
    all_to_all x1, starting transfers between devices, body(): slabs = lax.all_to_all(slabs, ('gz', 'gy'), 0, 0, tiled=True)  5.91 us
    ppermute x1, starting transfers between devices, body(): lax.ppermute(jnp.where(column_idx == 0, low_end, high_end), 'gx', [(0, 1)...  2.97 us
    pallas_call x1, Pallas kernels, body(): pl.pallas_call(weights_kernel, out_shape=shapes, in_specs=[vmem(), vmem()...  2.25 us
  transfers between devices with their start and end apart: 2, of which 0 were waited for; matrix products, arithmetic and copies ran while one was open for 17% of the time, Pallas kernels for 2%

commit v1 on v0

v1 whole, which is shorter than its diff:
```python
import functools

import jax
import jax.numpy as jnp
from jax import lax
from jax.experimental import pallas as pl
from jax.experimental.pallas import tpu as pltpu
from jax.sharding import PartitionSpec as P

LAYERS = 4
H = 64
S = 32
BX = 128
C = 32
REACH = 16
SLAB = 8
WIDE = SLAB + 2 * REACH
NZ = 32
NY = 32
GROUPS = (10, 9, 8, 6, 2)
TAPS = (2, 2, 3, 3)
STEP = (1, 1, 1, 2)
ORIGIN = (-15, -14, -12, -8, 0)
BF = jnp.bfloat16
F32 = jnp.float32


def repeated(row, copies):
    return jnp.concatenate([row] * copies, axis=1)


def weights_kernel(
    lw_ref, lb_ref, sw_ref, sb_ref, head_ref, rows_ref, ws_ref, w0, w1, w2, w3, turned
):
    w_refs = (w0, w1, w2, w3)
    lane = lax.broadcasted_iota(jnp.int32, (C, 4 * C), 1) // C
    zero = jnp.zeros((C, 4 * C), BF)
    for layer in range(LAYERS):
        spacing = 2**layer
        out = w_refs[layer]
        flat = lw_ref[layer].astype(F32).reshape(27 * C, C)
        flat = jnp.concatenate([flat, jnp.zeros((28 * 4 * C - 27 * C, C), F32)], axis=0)
        flat = jnp.concatenate([flat, jnp.zeros((28 * 4 * C, 3 * C), F32)], axis=1)
        for t in range(27):
            turned[t] = flat[C * t : C * t + 4 * C].T[:C]

        def per_row_tap(s, carry, layer=layer, spacing=spacing, out=out):
            taps = []
            for c in range(3):
                taps.append([])
                for a in range(3):
                    block = jnp.where(lane == 0, turned[9 * c + a + 3 * s], 0.0)
                    block = block + pltpu.roll(block, 2 * C, 1)
                    taps[c].append(block + pltpu.roll(block, C, 1))
            for i in range(TAPS[layer]):
                for xi in range(4):
                    rows = pl.ds(xi * C, C)
                    for c in range(3):
                        block = jnp.zeros((C, 4 * C), F32)
                        for a in range(3):
                            xo = 4 * STEP[layer] * i + xi - spacing * a
                            if 0 <= xo < 4:
                                block = jnp.where(lane == xo, taps[c][a], block)
                        block = block.astype(BF)
                        out[s, i, c, rows, 0 : 4 * C] = block
                        out[s, i, c + 1, rows, 4 * C : 8 * C] = block
                    out[s, i, 0, rows, 4 * C : 8 * C] = zero
                    out[s, i, 3, rows, 0 : 4 * C] = zero
            return carry

        lax.fori_loop(0, 3, per_row_tap, 0)
    row = lax.broadcasted_iota(jnp.int32, (128, 8 * C), 0)
    column = lax.broadcasted_iota(jnp.int32, (128, 8 * C), 1) // C
    stem = repeated(sw_ref[...].astype(F32), 8)

    def per_tile(k, carry):
        diff = row - column - 8 * k
        for c in range(3):
            block = jnp.zeros((128, 8 * C), F32)
            for b in range(3):
                for a in range(3):
                    tap = 9 * c + 3 * b + a
                    block = jnp.where(diff == WIDE * b + a, stem[tap : tap + 1, :], block)
            ws_ref[k, 128 * c : 128 * (c + 1), :] = block.astype(BF)
        return carry

    lax.fori_loop(0, GROUPS[0] // 2, per_tile, 0)
    rows_ref[...] = jnp.zeros(rows_ref.shape, F32)
    rows_ref[0:1, :] = repeated(sb_ref[...], 8)
    for layer in range(LAYERS):
        rows_ref[8 + layer : 9 + layer, :] = repeated(lb_ref[layer : layer + 1], 8)
    head = repeated(head_ref[...].astype(F32), 8)
    spot = lax.broadcasted_iota(jnp.int32, (8, 8 * C), 0)
    rows_ref[16:24, :] = jnp.where(spot == column[:8], head, 0.0)


def pack_kernel(off_ref, stacks_ref, out_ref, *, parts, bricks):
    brick = lax.axis_index("gx")
    tile_len = stacks_ref.shape[2]
    rows = out_ref.shape[1]
    values = stacks_ref[...].astype(F32).reshape(2 * rows, tile_len)
    lane = lax.broadcasted_iota(jnp.int32, (rows, 128), 1)
    for other in range(bricks):
        first = other * BX - REACH - (brick * BX - H + off_ref[brick])
        moved = pltpu.roll(values, lax.rem(64 * tile_len - first, tile_len), 1)
        for j in range(parts):
            low = pltpu.roll(moved[:rows], (tile_len - SLAB * j) % tile_len, 1)[:, :128]
            high = pltpu.roll(moved[rows:], (tile_len + 64 - SLAB * j) % tile_len, 1)[:, :128]
            out_ref[j * bricks + other] = jnp.where(lane < 64, low, high).astype(BF)


def unpack_kernel(pieces_ref, out_ref):
    out_ref[...] = pieces_ref[...].reshape(128, 128).T[: out_ref.shape[0]]


def blended_slab(off_ref, ramp_ref, pieces_ref, first_col, total_cols, depth_parts, row_parts):
    bricks = lax.axis_size("gx")
    brick = lax.axis_index("gx")
    lane = lax.broadcasted_iota(jnp.int32, (1, 128), 1) % 64
    col = lane + (first_col - REACH)
    numerator = jnp.zeros((depth_parts, row_parts, 32, 128), F32)
    denominator = jnp.zeros((1, 128), F32)
    for step in range(min(bricks, 3)):
        if bricks > 3:
            tile = jnp.clip(brick - 1 + step, 0, bricks - 1)
            real = (brick - 1 + step >= 0) & (brick - 1 + step < bricks)
        else:
            tile, real = step, True
        tile_len = 2 * BX
        spot = col - (tile * BX - H + off_ref[tile])
        inside = (spot >= 0) & (spot < tile_len) & real
        width = ramp_ref[tile].astype(F32)
        spot = spot.astype(F32)
        weight = jnp.minimum(1.0, jnp.minimum((spot + 1.0) / width, (tile_len - spot) / width))
        weight = jnp.where(inside, weight, 0.0)
        denominator = denominator + weight
        values = pieces_ref[:, :, tile].astype(F32)
        numerator = numerator + values * weight
    good = (col >= 0) & (col < total_cols)
    result = jnp.where(good, numerator / jnp.where(good, denominator, 1.0), 0.0)
    zrows = result.reshape(depth_parts, row_parts, 4, 8, 128)
    low = zrows.transpose(0, 2, 1, 3, 4)
    high = pltpu.roll(result.reshape(-1, 128), 64, 1).reshape(zrows.shape).transpose(0, 2, 1, 3, 4)
    image = jnp.stack([low, high], axis=1).reshape(NZ * NY, 128)
    lanes = lax.broadcasted_iota(jnp.int32, image.shape, 1)
    return jnp.where(lanes < WIDE, image, 0.0)


def shifted(value, by):
    rows = value.shape[0]
    spot = lax.broadcasted_iota(jnp.int32, value.shape, 0) % NY
    moved = pltpu.roll(value, by % rows, 0)
    keep = (spot >= by) if by > 0 else (spot < NY + by)
    return jnp.where(keep, moved, 0.0)


def conv_kernel(
    off_ref, ramp_ref, pieces_ref, rows_ref, ws_ref, w0, w1, w2, w3, out_ref, stem_in, *acts
):
    w_refs = (w0, w1, w2, w3)
    depth_parts, row_parts = lax.axis_size("gz"), lax.axis_size("gy")
    slab = lax.axis_index("gz") * row_parts + lax.axis_index("gy")
    first_col = lax.axis_index("gx") * BX + slab * SLAB
    total_cols = lax.axis_size("gx") * BX

    def col_mask(layer, group, width):
        lane = lax.broadcasted_iota(jnp.int32, (1, width * C), 1) // C
        col = lane + (4 * group + first_col + ORIGIN[layer])
        return jnp.where((col >= 0) & (col < total_cols), 1.0, 0.0)

    for layer in range(LAYERS):
        spacing = 2**layer
        pad = jnp.zeros((3, spacing, NY, 4 * C), BF)
        for g in range(GROUPS[layer]):
            acts[layer][:, g, 1, :, 0] = pad
            acts[layer][:, g, 0, :, NZ // (2 * spacing) + 1] = pad

    image = blended_slab(
        off_ref, ramp_ref, pieces_ref, first_col, total_cols, depth_parts, row_parts
    )
    packed = shifted(image, 1)
    packed = packed + pltpu.roll(image, WIDE, 1)
    packed = packed + pltpu.roll(shifted(image, -1), 2 * WIDE, 1)
    coarse = packed.astype(BF)
    fine = (packed - coarse.astype(F32)).astype(BF)
    for part, value in enumerate((coarse, fine)):
        stem_in[part, 0] = jnp.zeros((NY, 128), BF)
        stem_in[part, NZ + 1] = jnp.zeros((NY, 128), BF)
        stem_in[part, 1 : NZ + 1] = value.reshape(NZ, NY, 128)

    def store(layer, group, plane_sets):
        spacing = 2**layer
        for lead, value in plane_sets:
            for s in range(3):
                part = value if s == 1 else shifted(value, spacing if s == 0 else -spacing)
                planes = part.astype(BF).reshape(lead[1], NZ // (2 * spacing), 2, NY, 4 * C)
                for b in range(2):
                    acts[layer][
                        s, group, b, lead[0] : lead[0] + lead[1], 1 : 1 + NZ // (2 * spacing)
                    ] = planes[:, :, b]

    def stem_tile(k, carry):
        acc = jnp.zeros((NZ * NY, 8 * C), F32)
        lhs = jnp.concatenate(
            [stem_in[p, c : c + NZ].reshape(NZ * NY, 128) for p in range(2) for c in range(3)],
            axis=1,
        )
        weights = jnp.concatenate([ws_ref[k], ws_ref[k]], axis=0)
        acc = jnp.dot(lhs, weights, preferred_element_type=F32)
        acc = jnp.maximum(acc + rows_ref[0:1], 0.0) * col_mask(0, 2 * k, 8)
        store(0, 2 * k, [((0, 1), acc[:, : 4 * C])])
        store(0, 2 * k + 1, [((0, 1), acc[:, 4 * C :])])
        return carry

    lax.fori_loop(0, GROUPS[0] // 2, stem_tile, 0)

    for layer in range(LAYERS):
        spacing = 2**layer
        count = NZ // (2 * spacing)
        src = acts[layer]

        def conv_group(g, carry, layer=layer, spacing=spacing, count=count, src=src):
            pieces = []
            for s in range(3):
                for i in range(TAPS[layer]):
                    for t in range(4):
                        piece = src[
                            s,
                            g + STEP[layer] * i,
                            1 - t % 2,
                            :,
                            (t + 1) // 2 : (t + 1) // 2 + count,
                        ]
                        pieces.append(piece.reshape(NZ * NY // 2, 4 * C))
            lhs = jnp.concatenate(pieces, axis=1)
            weights = w_refs[layer][...].reshape(3 * TAPS[layer] * 4 * 128, 8 * C)
            acc = jnp.dot(lhs, weights, preferred_element_type=F32)
            mask = col_mask(layer + 1, g, 4)
            halves = []
            for b in range(2):
                if layer < 2:
                    pair = jnp.concatenate(
                        [
                            src[1, g + i, b, :, 1 : 1 + count].reshape(NZ * NY // 2, 4 * C)
                            for i in range(2)
                        ],
                        axis=1,
                    ).astype(F32)
                    centre = pair[:, spacing * C : spacing * C + 4 * C]
                else:
                    centre = src[1, g + STEP[layer], b, :, 1 : 1 + count]
                    centre = centre.reshape(NZ * NY // 2, 4 * C).astype(F32)
                half = acc[:, 4 * C * b : 4 * C * (b + 1)] + rows_ref[8 + layer : 9 + layer, : 4 * C]
                halves.append(centre + jnp.maximum(half, 0.0) * mask)
            if layer + 1 < LAYERS:
                store(layer + 1, g, [((spacing * b, spacing), halves[b]) for b in range(2)])
            else:
                last = jnp.concatenate(halves, axis=1)
                last = last.reshape(spacing, count, row_parts, NY // row_parts, 8 * C)
                last = last.transpose(1, 2, 0, 3, 4).reshape(NZ * NY // 2, 8 * C).astype(BF)
                heads = lax.dot_general(
                    rows_ref[16:24].astype(BF),
                    last,
                    (((1,), (1,)), ((), ())),
                    preferred_element_type=F32,
                )
                size = NZ * NY // 2 // (count * row_parts)
                for m in range(count):
                    for y in range(row_parts):
                        at = (m * row_parts + y) * size
                        for b in range(2):
                            out_ref[
                                (2 * m + b) * row_parts + y, pl.ds(4 * g, 4), 0:size
                            ] = heads[4 * b : 4 * b + 4, at : at + size]
            return carry

        if layer + 1 < LAYERS:
            lax.fori_loop(0, GROUPS[layer + 1], conv_group, 0)
        else:
            for g in range(GROUPS[layer + 1]):
                conv_group(g, 0)


def vmem():
    return pl.BlockSpec(memory_space=pltpu.VMEM)


def body(
    stacks, offsets, ramp_width, stem_weight, stem_bias, layer_weight, layer_bias, head_weight
):
    depth_b, rows_b, tile_len = stacks.shape
    depth_parts, row_parts = lax.axis_size("gz"), lax.axis_size("gy")
    parts = depth_parts * row_parts
    bricks = lax.axis_size("gx")
    assert (depth_b * depth_parts, rows_b * row_parts, parts * SLAB) == (NZ, NY, BX)
    half = depth_b * rows_b // 2
    smem = pl.BlockSpec(memory_space=pltpu.SMEM)
    pieces = pl.pallas_call(
        functools.partial(pack_kernel, parts=parts, bricks=bricks),
        out_shape=jax.ShapeDtypeStruct((parts * bricks, half, 128), BF),
        in_specs=[smem, vmem()],
        out_specs=vmem(),
    )(offsets, stacks)
    pieces = lax.all_to_all(pieces, ("gz", "gy", "gx"), 0, 0, tiled=True)
    pieces = pieces.reshape(depth_parts, row_parts, bricks, half, 128)

    shapes = [
        jax.ShapeDtypeStruct((24, 8 * C), F32),
        jax.ShapeDtypeStruct((GROUPS[0] // 2, 384, 8 * C), BF),
    ] + [
        jax.ShapeDtypeStruct((3, TAPS[layer], 4, 4 * C, 8 * C), BF) for layer in range(LAYERS)
    ]
    weights = pl.pallas_call(
        weights_kernel,
        out_shape=shapes,
        in_specs=[vmem()] * 5,
        out_specs=[vmem()] * 6,
        scratch_shapes=[pltpu.VMEM((27, C, 4 * C), F32)],
        compiler_params=pltpu.CompilerParams(vmem_limit_bytes=32 * 2**20),
        cost_estimate=pl.CostEstimate(flops=4000000, bytes_accessed=9000000, transcendentals=0),
    )(layer_weight, layer_bias, stem_weight, stem_bias[None], head_weight[None])

    scratch = [pltpu.VMEM((2, NZ + 2, NY, 128), BF)] + [
        pltpu.VMEM((3, GROUPS[layer], 2, 2**layer, NZ // 2 ** (layer + 1) + 2, NY, 4 * C), BF)
        for layer in range(LAYERS)
    ]
    logits = pl.pallas_call(
        conv_kernel,
        out_shape=jax.ShapeDtypeStruct((parts, SLAB, 128), F32),
        in_specs=[smem, smem] + [vmem()] * 7,
        out_specs=vmem(),
        scratch_shapes=scratch,
        compiler_params=pltpu.CompilerParams(vmem_limit_bytes=60 * 2**20),
        cost_estimate=pl.CostEstimate(
            flops=20000000000, bytes_accessed=9000000, transcendentals=0
        ),
    )(offsets, ramp_width, pieces, *weights)
    logits = lax.all_to_all(logits, ("gz", "gy"), 0, 0, tiled=True)
    logits = pl.pallas_call(
        unpack_kernel,
        out_shape=jax.ShapeDtypeStruct((depth_b * rows_b, BX), F32),
        in_specs=[vmem()],
        out_specs=vmem(),
    )(logits)
    return logits.reshape(depth_b, rows_b, BX)


def solution(mesh):
    return jax.shard_map(
        body,
        mesh=mesh,
        in_specs=(P("gz", "gy", "gx"), P(), P(), P(), P(), P(), P(), P()),
        out_specs=P("gz", "gy", "gx"),
        check_vma=False,
    )
```

time: 104 us -> 85.7 us (0.82)
  local copies, waits for them, and re-layouts: 24.9 us -> 11.4 us
  Pallas kernels: 44 us -> 53.6 us
  other arithmetic: 7.59 us -> 0 us
  between operations: 5.86 us -> 0.05 us
  starting transfers between devices: 8.88 us -> 7.3 us
    another operation x9 -> x0, local copies, waits for them, and re-layouts: 9.9 us -> none  [the longest x2 8.42 us: body(): tiled = jnp.tile(jnp.swapaxes(layer_weight, 2, 3), (1, 1, 1, 4))]
    pallas_call x2 -> x4, Pallas kernels: 44 us -> 53.6 us  [the longest x1 45.1 us: body(): pl.pallas_call(conv_kernel, out_shape=jax.ShapeDtypeStruct((parts, SLAB,...]
    ppermute x1 -> x0, starting transfers between devices: 2.97 us -> none  [body(): lax.ppermute(jnp.where(column_idx == 0, low_end, high_end), 'gx', [(0, 1)...]
    reshape x4 -> x0, local copies, waits for them, and re-layouts: 2.46 us -> none  [the longest x2 1.51 us: body(): flat.reshape(2, 2, 4, 8, 2, row_parts, rows_b)]
    unnamed x35 -> x24, local copies, waits for them, and re-layouts: 8.93 us -> 11.4 us
    transpose x2 -> x0, local copies, waits for them, and re-layouts: 2.19 us -> none  [the longest x1 1.5 us: body(): tiled = jnp.tile(jnp.swapaxes(layer_weight, 2, 3), (1, 1, 1, 4))]
    add x1 -> x0, other arithmetic: 1.91 us -> none  [body(): blended = numerator / (weight_own + weight_lower + weight_upper)]
    convert_element_type x3 -> x0, other arithmetic: 1.45 us -> none  [the longest x1 0.86 us: body(): blended = blended.astype(BF)]
  transfers between devices with their start and end apart: 2 -> 1, of which waited for: 0 -> 0; matrix products, arithmetic and copies ran while one was open for 17% -> 0% of each run, Pallas kernels for 2% -> 6%
where the time goes in v1:
time: 85.7 us; the launch traced here: 85.2 us
  Pallas kernels  53.6 us (63%)
  blocking collectives  12.9 us (15%)
  local copies, waits for them, and re-layouts  11.4 us (13%)
  starting transfers between devices  7.3 us (9%)
    pallas_call x1, Pallas kernels, body(): pl.pallas_call(conv_kernel, out_shape=jax.ShapeDtypeStruct((parts, SLAB,...  45.1 us
    all_to_all x1, blocking collectives, body(): logits = lax.all_to_all(logits, ('gz', 'gy'), 0, 0, tiled=True)  12.9 us
    unnamed x24, local copies, waits for them, and re-layouts  11.4 us
    all_to_all x1, starting transfers between devices, body(): pieces = lax.all_to_all(pieces, ('gz', 'gy', 'gx'), 0, 0, tiled=True)  7.3 us
    pallas_call x1, Pallas kernels, body(): pl.pallas_call(weights_kernel, out_shape=shapes, in_specs=[vmem()] * 5, o...  4.96 us
    pallas_call x1, Pallas kernels, body(): pl.pallas_call(functools.partial(pack_kernel, parts=parts, bricks=bricks)...  1.98 us
  transfers between devices with their start and end apart: 1, of which 0 were waited for; matrix products, arithmetic and copies ran while one was open for 0% of the time, Pallas kernels for 6%

profile of v1, /device:TPU:0, one launch (start us, length us, event | category | flops | bytes accessed | tf_op | source)
XLA Modules:
  0.0 85.2 jit_solution(15742096544280853051)
XLA Ops:
  0.0 2.0 %shard_map.82 = bf16[32,32,128]{2,1,0:T(8,128)(2,1)} custom-call(s32[2]{0:T(128)} %off_ref.3, bf16[8,8,256]{2,1,0:T(8,128)(2,1)} %stacks_ref.1), custom_call_target="tpu_custom_call" | custom-call | tf_op jit(solution)/shard_map/pallas_call | solution.py:298
  2.0 7.3 %all-to-all-start = ((bf16[32,32,128]{2,1,0:T(8,128)(2,1)}), bf16[32,32,128]{2,1,0:T(8,128)(2,1)S(1)}, u32[]{:S(2)}, u32[]{:S(2)}) async-start(bf16[32,32,128]{2,1,0:T(8,128)(2,1)} %shard_map.82), calls=%async_computation | async-start | bytes 524288 | tf_op jit(solution)/shard_map/all_to_all | solution.py:304
  9.3 0.0 copy-start
  9.3 1.2 %copy-done = bf16[4,27,32,32]{3,2,1,0:T(8,128)(2,1)S(1)} copy-done((bf16[4,27,32,32]{3,2,1,0:T(8,128)(2,1)S(1)}, bf16[4,27,32,32]{3,2,1,0:T(8,128)(2,1)}, u32[]{:S(2)}) %copy-start) | copy-done | bytes 221208
  10.5 0.0 copy-start.1
  10.5 0.7 copy-done.1
  11.2 0.0 copy-start.2
  11.2 0.7 copy-done.2
  11.8 0.0 copy-start.3
  11.8 0.7 copy-done.3
  12.5 0.0 copy-start.4
  12.5 0.7 copy-done.4
  13.1 5.0 %shard_map.83 = (f32[24,256]{1,0:T(8,128)S(1)}, bf16[5,384,256]{2,1,0:T(8,128)(2,1)S(1)}, bf16[3,2,4,128,256]{4,3,2,1,0:T(8,128)(2,1)S(1)}, bf16[3,2,4,128,256]{...) custom-call(bf16[4,27,32,32]{3,2,1,0:T(8,128)(2,1)S(1)} %copy-done, ...), custom_call_target="tpu_custom_call" | custom-call | flops 4000000 | bytes 9000000 | tf_op jit(solution)/shard_map/pallas_call | solution.py:313
  18.1 0.0 copy-start.5
  18.1 1.4 %copy-done.5 = bf16[3,3,4,128,256]{4,3,2,1,0:T(8,128)(2,1)} copy-done((bf16[3,3,4,128,256]{4,3,2,1,0:T(8,128)(2,1)}, bf16[3,3,4,128,256]{4,3,2,1,0:T(8,128)(2,1)S(1)}, u32[]{:S(2)}) %copy-start.5) | copy-done | bytes 2359320
  19.5 0.0 copy-start.6
  19.5 1.4 %copy-done.6 = bf16[3,3,4,128,256]{4,3,2,1,0:T(8,128)(2,1)} copy-done((bf16[3,3,4,128,256]{4,3,2,1,0:T(8,128)(2,1)}, bf16[3,3,4,128,256]{4,3,2,1,0:T(8,128)(2,1)S(1)}, u32[]{:S(2)}) %copy-start.6) | copy-done | bytes 2359320
  21.0 0.0 copy-start.7
  21.0 1.2 %copy-done.7 = bf16[3,2,4,128,256]{4,3,2,1,0:T(8,128)(2,1)} copy-done((bf16[3,2,4,128,256]{4,3,2,1,0:T(8,128)(2,1)}, bf16[3,2,4,128,256]{4,3,2,1,0:T(8,128)(2,1)S(1)}, u32[]{:S(2)}) %copy-start.7) | copy-done | bytes 1572888
  22.1 0.0 copy-start.8
  22.1 1.1 %copy-done.8 = bf16[3,2,4,128,256]{4,3,2,1,0:T(8,128)(2,1)} copy-done((bf16[3,2,4,128,256]{4,3,2,1,0:T(8,128)(2,1)}, bf16[3,2,4,128,256]{4,3,2,1,0:T(8,128)(2,1)S(1)}, u32[]{:S(2)}) %copy-start.8) | copy-done | bytes 1572888
  23.3 0.0 copy-start.9
  23.3 1.0 %copy-done.9 = bf16[5,384,256]{2,1,0:T(8,128)(2,1)} copy-done((bf16[5,384,256]{2,1,0:T(8,128)(2,1)}, bf16[5,384,256]{2,1,0:T(8,128)(2,1)S(1)}, u32[]{:S(2)}) %copy-start.9) | copy-done | bytes 983064
  24.3 0.0 copy-start.10
  24.3 0.6 copy-done.10
  24.9 0.0 all-to-all-done
  24.9 0.0 copy-start.11
  24.9 0.7 copy-done.11
  25.7 45.1 %shard_map.84 = f32[16,8,128]{2,1,0:T(8,128)} custom-call(s32[2]{0:T(128)} %off_ref.3, s32[2]{0:T(128)} %ramp_ref.1, bf16[4,4,2,32,128]{4,3,2,1,0:T(8,128)(2,1)} %bitcast.6, f32[24,256]{1,0:T(8,128)} %copy-done.10, bf16[5,384,256]{2,1,0:T(8,128)(2,1)} %copy-done.9, bf16[3,2,4,128,256]{4,3,2,1,0:T(8,128)(2,1)} %copy-done.7, ...), custom_call_target="tpu_custom_call" | custom-call | flops 20000000000 | bytes 9000000 | tf_op jit(solution)/shard_map/pallas_call | solution.py:327
  70.8 12.9 %all_to_all.10.pieces_ref = f32[16,8,128]{2,1,0:T(8,128)} all-to-all(f32[16,8,128]{2,1,0:T(8,128)} %shard_map.84), channel_id=1, replica_groups=mesh['gz'=4,'gy'=4,'gx'=2] {'gz','gy'}, dimensions={0} | all-to-all | bytes 131072 | tf_op jit(solution)/shard_map/all_to_all | solution.py:338
  83.7 1.5 %shard_map.85 = f32[64,128]{1,0:T(8,128)} custom-call(f32[16,8,128]{2,1,0:T(8,128)} %all_to_all.10.pieces_ref), custom_call_target="tpu_custom_call" | custom-call | tf_op jit(solution)/shard_map/pallas_call | solution.py:339
Async XLA Ops:
  2.0 23.0 %all-to-all-start = ((bf16[32,32,128]{2,1,0:T(8,128)(2,1)}), bf16[32,32,128]{2,1,0:T(8,128)(2,1)S(1)}, u32[]{:S(2)}, u32[]{:S(2)}) async-start(bf16[32,32,128]{2,1,0:T(8,128)(2,1)} %shard_map.82), calls=%async_computation | async-start | bytes 524288 | tf_op jit(solution)/shard_map/all_to_all | solution.py:304
  9.3 1.2 %copy-start = (bf16[4,27,32,32]{3,2,1,0:T(8,128)(2,1)S(1)}, bf16[4,27,32,32]{3,2,1,0:T(8,128)(2,1)}, u32[]{:S(2)}) copy-start(bf16[4,27,32,32]{3,2,1,0:T(8,128)(2,1)} %lw_ref.1) | copy-start | bytes 663556
  10.5 0.7 copy-start.1
  11.2 0.7 copy-start.2
  11.8 0.7 copy-start.3
  12.5 0.7 copy-start.4
  18.1 1.4 %copy-start.5 = (bf16[3,3,4,128,256]{4,3,2,1,0:T(8,128)(2,1)}, bf16[3,3,4,128,256]{4,3,2,1,0:T(8,128)(2,1)S(1)}, u32[]{:S(2)}) copy-start(bf16[3,3,4,128,256]{4,3,2,1,0:T(8,128)(2,1)S(1)} %get-tuple-element.15.w2) | copy-start | bytes 7077892
  19.5 1.4 %copy-start.6 = (bf16[3,3,4,128,256]{4,3,2,1,0:T(8,128)(2,1)}, bf16[3,3,4,128,256]{4,3,2,1,0:T(8,128)(2,1)S(1)}, u32[]{:S(2)}) copy-start(bf16[3,3,4,128,256]{4,3,2,1,0:T(8,128)(2,1)S(1)} %get-tuple-element.16.w3) | copy-start | bytes 7077892
  21.0 1.2 %copy-start.7 = (bf16[3,2,4,128,256]{4,3,2,1,0:T(8,128)(2,1)}, bf16[3,2,4,128,256]{4,3,2,1,0:T(8,128)(2,1)S(1)}, u32[]{:S(2)}) copy-start(bf16[3,2,4,128,256]{4,3,2,1,0:T(8,128)(2,1)S(1)} %get-tuple-element.13.w0) | copy-start | bytes 4718596
  22.1 1.2 %copy-start.8 = (bf16[3,2,4,128,256]{4,3,2,1,0:T(8,128)(2,1)}, bf16[3,2,4,128,256]{4,3,2,1,0:T(8,128)(2,1)S(1)}, u32[]{:S(2)}) copy-start(bf16[3,2,4,128,256]{4,3,2,1,0:T(8,128)(2,1)S(1)} %get-tuple-element.14.w1) | copy-start | bytes 4718596
  23.3 1.0 %copy-start.9 = (bf16[5,384,256]{2,1,0:T(8,128)(2,1)}, bf16[5,384,256]{2,1,0:T(8,128)(2,1)S(1)}, u32[]{:S(2)}) copy-start(bf16[5,384,256]{2,1,0:T(8,128)(2,1)S(1)} %get-tuple-element.12.ws_ref) | copy-start | bytes 2949124
  24.3 0.6 copy-start.10
  24.9 0.7 copy-start.11

commit v2 on v1

--- a/solution.py
+++ b/solution.py
@@ -1,4 +1,5 @@
 import functools
+import math
 
 import jax
 import jax.numpy as jnp
@@ -29,10 +30,21 @@
     return jnp.concatenate([row] * copies, axis=1)
 
 
-def weights_kernel(
-    lw_ref, lb_ref, sw_ref, sb_ref, head_ref, rows_ref, ws_ref, w0, w1, w2, w3, turned
-):
-    w_refs = (w0, w1, w2, w3)
+def weights_kernel(*refs):
+    sources, rows_ref, outs, refs = refs[:5], refs[5], refs[6:11], refs[11:]
+    inputs, built, turned, in_sems, out_sems = refs[:5], refs[5:10], *refs[10:]
+    fetches = [
+        pltpu.make_async_copy(a, b, in_sems.at[k]) for k, (a, b) in enumerate(zip(sources, inputs))
+    ]
+    stores = [
+        pltpu.make_async_copy(a, b, out_sems.at[k]) for k, (a, b) in enumerate(zip(built, outs))
+    ]
+    for copy in fetches:
+        copy.start()
+    for copy in fetches:
+        copy.wait()
+    lw_ref, lb_ref, sw_ref, sb_ref, head_ref = inputs
+    ws_ref, w_refs = built[0], built[1:]
     lane = lax.broadcasted_iota(jnp.int32, (C, 4 * C), 1) // C
     zero = jnp.zeros((C, 4 * C), BF)
     for layer in range(LAYERS):
@@ -69,6 +81,7 @@
             return carry
 
         lax.fori_loop(0, 3, per_row_tap, 0)
+        stores[1 + layer].start()
     row = lax.broadcasted_iota(jnp.int32, (128, 8 * C), 0)
     column = lax.broadcasted_iota(jnp.int32, (128, 8 * C), 1) // C
     stem = repeated(sw_ref[...].astype(F32), 8)
@@ -85,6 +98,7 @@
         return carry
 
     lax.fori_loop(0, GROUPS[0] // 2, per_tile, 0)
+    stores[0].start()
     rows_ref[...] = jnp.zeros(rows_ref.shape, F32)
     rows_ref[0:1, :] = repeated(sb_ref[...], 8)
     for layer in range(LAYERS):
@@ -92,6 +106,8 @@
     head = repeated(head_ref[...].astype(F32), 8)
     spot = lax.broadcasted_iota(jnp.int32, (8, 8 * C), 0)
     rows_ref[16:24, :] = jnp.where(spot == column[:8], head, 0.0)
+    for copy in stores:
+        copy.wait()
 
 
 def pack_kernel(off_ref, stacks_ref, out_ref, *, parts, bricks):
@@ -154,10 +170,27 @@
     return jnp.where(keep, moved, 0.0)
 
 
-def conv_kernel(
-    off_ref, ramp_ref, pieces_ref, rows_ref, ws_ref, w0, w1, w2, w3, out_ref, stem_in, *acts
-):
-    w_refs = (w0, w1, w2, w3)
+def act_shape(layer):
+    return (3, GROUPS[layer], 2, 2**layer, NZ // 2 ** (layer + 1) + 2, NY, 4 * C)
+
+
+def act_rows(layer):
+    return math.prod(act_shape(layer)[:-2])
+
+
+def conv_kernel(off_ref, ramp_ref, pieces_ref, rows_ref, *refs):
+    built, out_ref, refs = refs[:5], refs[5], refs[6:]
+    held, stem_in, spaces, accs, sems = refs[:5], refs[5], refs[6:8], refs[8:10], refs[10]
+    fetches = [
+        pltpu.make_async_copy(a, b, sems.at[k]) for k, (a, b) in enumerate(zip(built, held))
+    ]
+    for copy in fetches:
+        copy.start()
+    ws_ref, w_refs = held[0], held[1:]
+    acts = [
+        spaces[layer % 2].at[0 : act_rows(layer)].reshape(act_shape(layer))
+        for layer in range(LAYERS)
+    ]
     depth_parts, row_parts = lax.axis_size("gz"), lax.axis_size("gy")
     slab = lax.axis_index("gz") * row_parts + lax.axis_index("gy")
     first_col = lax.axis_index("gx") * BX + slab * SLAB
@@ -168,13 +201,31 @@
         col = lane + (4 * group + first_col + ORIGIN[layer])
         return jnp.where((col >= 0) & (col < total_cols), 1.0, 0.0)
 
-    for layer in range(LAYERS):
+    def clear_edges(layer):
         spacing = 2**layer
         pad = jnp.zeros((3, spacing, NY, 4 * C), BF)
         for g in range(GROUPS[layer]):
             acts[layer][:, g, 1, :, 0] = pad
             acts[layer][:, g, 0, :, NZ // (2 * spacing) + 1] = pad
 
+    def store(layer, group, start, length, value):
+        spacing = 2**layer
+        for s in range(3):
+            part = value if s == 1 else shifted(value, spacing if s == 0 else -spacing)
+            planes = part.astype(BF).reshape(length, -1, 2, NY, 4 * C)
+            for b in range(2):
+                acts[layer][s, group, b, start : start + length, 1 : 1 + planes.shape[1]] = planes[
+                    :, :, b
+                ]
+
+    def store_plane(layer, group, start, length, m, value):
+        spacing = 2**layer
+        for s in range(3):
+            part = value if s == 1 else shifted(value, spacing if s == 0 else -spacing)
+            planes = part.astype(BF).reshape(length, NY, 4 * C)
+            acts[layer][s, group, m % 2, start : start + length, 1 + m // 2] = planes
+
+    clear_edges(0)
     image = blended_slab(
         off_ref, ramp_ref, pieces_ref, first_col, total_cols, depth_parts, row_parts
     )
@@ -188,97 +239,135 @@
         stem_in[part, NZ + 1] = jnp.zeros((NY, 128), BF)
         stem_in[part, 1 : NZ + 1] = value.reshape(NZ, NY, 128)
 
-    def store(layer, group, plane_sets):
-        spacing = 2**layer
-        for lead, value in plane_sets:
-            for s in range(3):
-                part = value if s == 1 else shifted(value, spacing if s == 0 else -spacing)
-                planes = part.astype(BF).reshape(lead[1], NZ // (2 * spacing), 2, NY, 4 * C)
-                for b in range(2):
-                    acts[layer][
-                        s, group, b, lead[0] : lead[0] + lead[1], 1 : 1 + NZ // (2 * spacing)
-                    ] = planes[:, :, b]
-
-    def stem_tile(k, carry):
-        acc = jnp.zeros((NZ * NY, 8 * C), F32)
+    def stem_dot(k):
         lhs = jnp.concatenate(
             [stem_in[p, c : c + NZ].reshape(NZ * NY, 128) for p in range(2) for c in range(3)],
             axis=1,
         )
         weights = jnp.concatenate([ws_ref[k], ws_ref[k]], axis=0)
-        acc = jnp.dot(lhs, weights, preferred_element_type=F32)
-        acc = jnp.maximum(acc + rows_ref[0:1], 0.0) * col_mask(0, 2 * k, 8)
-        store(0, 2 * k, [((0, 1), acc[:, : 4 * C])])
-        store(0, 2 * k + 1, [((0, 1), acc[:, 4 * C :])])
-        return carry
-
-    lax.fori_loop(0, GROUPS[0] // 2, stem_tile, 0)
-
+        return jnp.dot(lhs, weights, preferred_element_type=F32)
+
+    def stem_finish(k, acc):
+        value = jnp.maximum(acc + rows_ref[0:1], 0.0) * col_mask(0, 2 * k, 8)
+        store(0, 2 * k, 0, 1, value[:, : 4 * C])
+        store(0, 2 * k + 1, 0, 1, value[:, 4 * C :])
+
+    def group_dot(layer, g):
+        spacing = 2**layer
+        count = NZ // (2 * spacing)
+        pieces = []
+        for s in range(3):
+            for i in range(TAPS[layer]):
+                for t in range(4):
+                    start = (t + 1) // 2
+                    piece = acts[layer][s, g + i, 1 - t % 2, :, start : start + count]
+                    pieces.append(piece.reshape(NZ * NY // 2, 4 * C))
+        lhs = jnp.concatenate(pieces, axis=1)
+        weights = w_refs[layer][...].reshape(12 * TAPS[layer] * 4 * C, 8 * C)
+        return jnp.dot(lhs, weights, preferred_element_type=F32)
+
+    def group_finish(layer, g, acc):
+        spacing = 2**layer
+        count = NZ // (2 * spacing)
+        mask = col_mask(layer + 1, g, 4)
+        bias = rows_ref[8 + layer : 9 + layer, : 4 * C]
+        for b in range(2):
+            pair = jnp.concatenate(
+                [
+                    acts[layer][1, g + i, b, :, 1 : 1 + count].reshape(NZ * NY // 2, 4 * C)
+                    for i in range(2)
+                ],
+                axis=1,
+            ).astype(F32)
+            centre = pair[:, spacing * C : spacing * C + 4 * C]
+            half = acc[0 : NZ * NY // 2, 4 * C * b : 4 * C * (b + 1)] + bias
+            value = centre + jnp.maximum(half, 0.0) * mask
+            store(layer + 1, g, spacing * b, spacing, value)
+
+    def plane_dot(layer, m):
+        spacing = 2**layer
+        groups = GROUPS[layer + 1]
+        taps = [t for t in range(4) if 0 < m + (t + 1) // 2 < NZ // (2 * spacing) + 1]
+        pieces, weights = [], []
+        for s in range(3):
+            for i in range(TAPS[layer]):
+                for t in taps:
+                    first = STEP[layer] * i
+                    piece = acts[layer][s, first : first + groups, 1 - t % 2, :, m + (t + 1) // 2]
+                    pieces.append(piece.reshape(groups * spacing * NY, 4 * C))
+                    weights.append(w_refs[layer][s, i, t])
+        return jnp.dot(
+            jnp.concatenate(pieces, axis=1),
+            jnp.concatenate(weights, axis=0),
+            preferred_element_type=F32,
+        )
+
+    def plane_values(layer, m, g, acc):
+        spacing = 2**layer
+        rows = spacing * NY
+        mask = col_mask(layer + 1, g, 4)
+        bias = rows_ref[8 + layer : 9 + layer, : 4 * C]
+        values = []
+        for b in range(2):
+            centre = acts[layer][1, g + STEP[layer], b, :, 1 + m].reshape(rows, 4 * C)
+            half = acc[g * rows : (g + 1) * rows, 4 * C * b : 4 * C * (b + 1)] + bias
+            values.append(centre.astype(F32) + jnp.maximum(half, 0.0) * mask)
+        return values
+
+    def plane_finish(layer, m, acc):
+        spacing = 2**layer
+        for g in range(GROUPS[layer + 1]):
+            for b, value in enumerate(plane_values(layer, m, g, acc)):
+                store_plane(layer + 1, g, spacing * b, spacing, m, value)
+
+    def head_finish(m, acc):
+        layer = LAYERS - 1
+        spacing = 2**layer
+        for g in range(GROUPS[layer + 1]):
+            last = jnp.concatenate(plane_values(layer, m, g, acc), axis=1)
+            last = last.reshape(spacing, row_parts, NY // row_parts, 8 * C)
+            last = last.transpose(1, 0, 2, 3).reshape(spacing * NY, 8 * C).astype(BF)
+            heads = lax.dot_general(
+                rows_ref[16:24].astype(BF),
+                last,
+                (((1,), (1,)), ((), ())),
+                preferred_element_type=F32,
+            )
+            size = spacing * NY // row_parts
+            for y in range(row_parts):
+                for b in range(2):
+                    out_ref[(2 * m + b) * row_parts + y, 4 * g : 4 * g + 4, 0:size] = heads[
+                        4 * b : 4 * b + 4, y * size : (y + 1) * size
+                    ]
+
+    def in_line(count, dot, finish):
+        for k in range(count):
+            finish(k, dot(k))
+
+    fetches[0].wait()
+    in_line(GROUPS[0] // 2, stem_dot, stem_finish)
     for layer in range(LAYERS):
-        spacing = 2**layer
-        count = NZ // (2 * spacing)
-        src = acts[layer]
-
-        def conv_group(g, carry, layer=layer, spacing=spacing, count=count, src=src):
-            pieces = []
-            for s in range(3):
-                for i in range(TAPS[layer]):
-                    for t in range(4):
-                        piece = src[
-                            s,
-                            g + STEP[layer] * i,
-                            1 - t % 2,
-                            :,
-                            (t + 1) // 2 : (t + 1) // 2 + count,
-                        ]
-                        pieces.append(piece.reshape(NZ * NY // 2, 4 * C))
-            lhs = jnp.concatenate(pieces, axis=1)
-            weights = w_refs[layer][...].reshape(3 * TAPS[layer] * 4 * 128, 8 * C)
-            acc = jnp.dot(lhs, weights, preferred_element_type=F32)
-            mask = col_mask(layer + 1, g, 4)
-            halves = []
-            for b in range(2):
-                if layer < 2:
-                    pair = jnp.concatenate(
-                        [
-                            src[1, g + i, b, :, 1 : 1 + count].reshape(NZ * NY // 2, 4 * C)
-                            for i in range(2)
-                        ],
-                        axis=1,
-                    ).astype(F32)
-                    centre = pair[:, spacing * C : spacing * C + 4 * C]
-                else:
-                    centre = src[1, g + STEP[layer], b, :, 1 : 1 + count]
-                    centre = centre.reshape(NZ * NY // 2, 4 * C).astype(F32)
-                half = acc[:, 4 * C * b : 4 * C * (b + 1)] + rows_ref[8 + layer : 9 + layer, : 4 * C]
-                halves.append(centre + jnp.maximum(half, 0.0) * mask)
-            if layer + 1 < LAYERS:
-                store(layer + 1, g, [((spacing * b, spacing), halves[b]) for b in range(2)])
-            else:
-                last = jnp.concatenate(halves, axis=1)
-                last = last.reshape(spacing, count, row_parts, NY // row_parts, 8 * C)
-                last = last.transpose(1, 2, 0, 3, 4).reshape(NZ * NY // 2, 8 * C).astype(BF)
-                heads = lax.dot_general(
-                    rows_ref[16:24].astype(BF),
-                    last,
-                    (((1,), (1,)), ((), ())),
-                    preferred_element_type=F32,
-                )
-                size = NZ * NY // 2 // (count * row_parts)
-                for m in range(count):
-                    for y in range(row_parts):
-                        at = (m * row_parts + y) * size
-                        for b in range(2):
-                            out_ref[
-                                (2 * m + b) * row_parts + y, pl.ds(4 * g, 4), 0:size
-                            ] = heads[4 * b : 4 * b + 4, at : at + size]
-            return carry
-
+        fetches[1 + layer].wait()
         if layer + 1 < LAYERS:
-            lax.fori_loop(0, GROUPS[layer + 1], conv_group, 0)
+            clear_edges(layer + 1)
+        if layer < 2:
+            in_line(
+                GROUPS[layer + 1],
+                functools.partial(group_dot, layer),
+                functools.partial(group_finish, layer),
+            )
+        elif layer + 1 < LAYERS:
+            in_line(
+                NZ // 2 ** (layer + 1),
+                functools.partial(plane_dot, layer),
+                functools.partial(plane_finish, layer),
+            )
         else:
-            for g in range(GROUPS[layer + 1]):
-                conv_group(g, 0)
+            for m in range(NZ // 2 ** (layer + 1)):
+                accs[m][...] = plane_dot(layer, m)
+                if m:
+                    head_finish(m - 1, accs[m - 1])
+            head_finish(m, accs[m])
 
 
 def vmem():
@@ -304,37 +393,48 @@
     pieces = lax.all_to_all(pieces, ("gz", "gy", "gx"), 0, 0, tiled=True)
     pieces = pieces.reshape(depth_parts, row_parts, bricks, half, 128)
 
-    shapes = [
-        jax.ShapeDtypeStruct((24, 8 * C), F32),
-        jax.ShapeDtypeStruct((GROUPS[0] // 2, 384, 8 * C), BF),
-    ] + [
+    hbm = pl.BlockSpec(memory_space=pltpu.HBM)
+    small = jax.ShapeDtypeStruct((24, 8 * C), F32)
+    shapes = [jax.ShapeDtypeStruct((GROUPS[0] // 2, 384, 8 * C), BF)] + [
         jax.ShapeDtypeStruct((3, TAPS[layer], 4, 4 * C, 8 * C), BF) for layer in range(LAYERS)
     ]
-    weights = pl.pallas_call(
+    spaces = [pltpu.VMEM(shape.shape, shape.dtype) for shape in shapes]
+    raw = (layer_weight, layer_bias, stem_weight, stem_bias[None], head_weight[None])
+    rows, *weights = pl.pallas_call(
         weights_kernel,
-        out_shape=shapes,
-        in_specs=[vmem()] * 5,
-        out_specs=[vmem()] * 6,
-        scratch_shapes=[pltpu.VMEM((27, C, 4 * C), F32)],
-        compiler_params=pltpu.CompilerParams(vmem_limit_bytes=32 * 2**20),
+        out_shape=[small] + shapes,
+        in_specs=[hbm] * 5,
+        out_specs=[vmem()] + [hbm] * 5,
+        scratch_shapes=[pltpu.VMEM(array.shape, array.dtype) for array in raw]
+        + spaces
+        + [
+            pltpu.VMEM((27, C, 4 * C), F32),
+            pltpu.SemaphoreType.DMA((5,)),
+            pltpu.SemaphoreType.DMA((5,)),
+        ],
+        compiler_params=pltpu.CompilerParams(vmem_limit_bytes=64 * 2**20 - 2**18),
         cost_estimate=pl.CostEstimate(flops=4000000, bytes_accessed=9000000, transcendentals=0),
-    )(layer_weight, layer_bias, stem_weight, stem_bias[None], head_weight[None])
-
-    scratch = [pltpu.VMEM((2, NZ + 2, NY, 128), BF)] + [
-        pltpu.VMEM((3, GROUPS[layer], 2, 2**layer, NZ // 2 ** (layer + 1) + 2, NY, 4 * C), BF)
-        for layer in range(LAYERS)
-    ]
+    )(*raw)
+
+    held = [max(act_rows(layer) for layer in range(odd, LAYERS, 2)) for odd in range(2)]
+    scratch = (
+        spaces
+        + [pltpu.VMEM((2, NZ + 2, NY, 128), BF)]
+        + [pltpu.VMEM((size, NY, 4 * C), BF) for size in held]
+        + [pltpu.VMEM((NZ * NY // 2, 8 * C), F32)] * 2
+        + [pltpu.SemaphoreType.DMA((5,))]
+    )
     logits = pl.pallas_call(
         conv_kernel,
         out_shape=jax.ShapeDtypeStruct((parts, SLAB, 128), F32),
-        in_specs=[smem, smem] + [vmem()] * 7,
+        in_specs=[smem, smem, vmem(), vmem()] + [hbm] * 5,
         out_specs=vmem(),
         scratch_shapes=scratch,
-        compiler_params=pltpu.CompilerParams(vmem_limit_bytes=60 * 2**20),
+        compiler_params=pltpu.CompilerParams(vmem_limit_bytes=64 * 2**20 - 2**18),
         cost_estimate=pl.CostEstimate(
             flops=20000000000, bytes_accessed=9000000, transcendentals=0
         ),
-    )(offsets, ramp_width, pieces, *weights)
+    )(offsets, ramp_width, pieces, rows, *weights)
     logits = lax.all_to_all(logits, ("gz", "gy"), 0, 0, tiled=True)
     logits = pl.pallas_call(
         unpack_kernel,

time: 85.7 us -> 64.9 us (0.76)
  local copies, waits for them, and re-layouts: 11.4 us -> 0 us
  Pallas kernels: 53.6 us -> 43.1 us
  waiting for transfers between devices: 0.01 us -> 2.84 us
  blocking collectives: 12.9 us -> 11.1 us
    pallas_call x1, Pallas kernels: 45.1 us -> 31.8 us  [body(): pl.pallas_call(conv_kernel, out_shape=jax.ShapeDtypeStruct((parts, SLAB,...]
    unnamed x24 -> x0, local copies, waits for them, and re-layouts: 11.4 us -> none
    pallas_call x1, Pallas kernels: 4.96 us -> 7.82 us  [body(): pl.pallas_call(weights_kernel, out_shape=[small] + shapes, in_specs=[hbm]...]
    all_to_all x1, waiting for transfers between devices: 0.01 us -> 2.84 us  [body(): pieces = lax.all_to_all(pieces, ('gz', 'gy', 'gx'), 0, 0, tiled=True)]
    all_to_all x1, blocking collectives: 12.9 us -> 11.1 us  [body(): logits = lax.all_to_all(logits, ('gz', 'gy'), 0, 0, tiled=True)]
  transfers between devices with their start and end apart: 1 -> 1, of which waited for: 0 -> 1; matrix products, arithmetic and copies ran while one was open for 0% -> 0% of each run, Pallas kernels for 6% -> 12%
where the time goes in v2:
time: 64.9 us; the launch traced here: 64.5 us
  Pallas kernels  43.1 us (66%)
  blocking collectives  11.1 us (17%)
  starting transfers between devices  7.43 us (11%)
  waiting for transfers between devices  2.84 us (4%)
    pallas_call x1, Pallas kernels, body(): pl.pallas_call(conv_kernel, out_shape=jax.ShapeDtypeStruct((parts, SLAB,...  31.8 us
    all_to_all x1, blocking collectives, body(): logits = lax.all_to_all(logits, ('gz', 'gy'), 0, 0, tiled=True)  11.1 us
    pallas_call x1, Pallas kernels, body(): pl.pallas_call(weights_kernel, out_shape=[small] + shapes, in_specs=[hbm]...  7.82 us
    all_to_all x1, starting transfers between devices, body(): pieces = lax.all_to_all(pieces, ('gz', 'gy', 'gx'), 0, 0, tiled=True)  7.43 us
    all_to_all x1, waiting for transfers between devices, body(): pieces = lax.all_to_all(pieces, ('gz', 'gy', 'gx'), 0, 0, tiled=True)  2.84 us
    pallas_call x1, Pallas kernels, body(): pl.pallas_call(functools.partial(pack_kernel, parts=parts, bricks=bricks)...  2 us
    pallas_call x1, Pallas kernels, body(): pl.pallas_call(unpack_kernel, out_shape=jax.ShapeDtypeStruct((depth_b * r...  1.54 us
  transfers between devices with their start and end apart: 1, of which 1 were waited for; matrix products, arithmetic and copies ran while one was open for 0% of the time, Pallas kernels for 12%

profile of v2, /device:TPU:0, one launch (start us, length us, event | category | flops | bytes accessed | tf_op | source)
XLA Modules:
  0.0 64.5 jit_solution(6789969780607096359)
XLA Ops:
  0.0 2.0 %shard_map.82 = bf16[32,32,128]{2,1,0:T(8,128)(2,1)} custom-call(s32[2]{0:T(128)} %off_ref.3, bf16[8,8,256]{2,1,0:T(8,128)(2,1)} %stacks_ref.1), custom_call_target="tpu_custom_call" | custom-call | tf_op jit(solution)/shard_map/pallas_call | solution.py:387
  2.0 7.4 %all-to-all-start = ((bf16[32,32,128]{2,1,0:T(8,128)(2,1)}), bf16[32,32,128]{2,1,0:T(8,128)(2,1)}, u32[]{:S(2)}, u32[]{:S(2)}) async-start(bf16[32,32,128]{2,1,0:T(8,128)(2,1)} %shard_map.82), calls=%async_computation | async-start | bytes 524288 | tf_op jit(solution)/shard_map/all_to_all | solution.py:393
  9.4 7.8 %shard_map.83 = (f32[24,256]{1,0:T(8,128)}, bf16[5,384,256]{2,1,0:T(8,128)(2,1)}, bf16[3,2,4,128,256]{4,3,2,1,0:T(8,128)(2,1)}, bf16[3,2,4,128,256]{4,3,2,1,0:T(...) custom-call(bf16[4,27,32,32]{3,2,1,0:T(8,128)(2,1)} %refs_0_.1, f32[4,32]{1,0:T(4,128)} %refs_1_.1, ...), custom_call_target="tpu_custom_call" | custom-call | flops 4000000 | bytes 9000000 | tf_op jit(solution)/shard_map/pallas_call | solution.py:403
  17.3 2.8 %all-to-all-done = bf16[32,32,128]{2,1,0:T(8,128)(2,1)} async-done(((bf16[32,32,128]{2,1,0:T(8,128)(2,1)}), bf16[32,32,128]{2,1,0:T(8,128)(2,1)}, u32[]{:S(2)}, u32[]{:S(2)}) %all-to-all-start) | async-done | bytes 262176 | tf_op jit(solution)/shard_map/all_to_all | solution.py:393
  20.1 31.8 %shard_map.84 = f32[16,8,128]{2,1,0:T(8,128)} custom-call(s32[2]{0:T(128)} %off_ref.3, s32[2]{0:T(128)} %ramp_ref.1, bf16[4,4,2,32,128]{4,3,2,1,0:T(8,128)(2,1)} %bitcast.pieces_ref, f32[24,256]{1,0:T(8,128)} %get-tuple-element.11.rows_ref, bf16[5,384,256]{2,1,0:T(8,128)(2,1)} %get-tuple-element.12.refs_0_, ...), custom_call_target="tpu_custom_call" | custom-call | flops 20000000000 | bytes 9000000 | tf_op jit(solution)/shard_map/pallas_call | solution.py:427
  51.9 11.1 %all_to_all.10.pieces_ref = f32[16,8,128]{2,1,0:T(8,128)} all-to-all(f32[16,8,128]{2,1,0:T(8,128)} %shard_map.84), channel_id=1, replica_groups=mesh['gz'=4,'gy'=4,'gx'=2] {'gz','gy'}, dimensions={0} | all-to-all | bytes 131072 | tf_op jit(solution)/shard_map/all_to_all | solution.py:438
  62.9 1.5 %shard_map.85 = f32[64,128]{1,0:T(8,128)} custom-call(f32[16,8,128]{2,1,0:T(8,128)} %all_to_all.10.pieces_ref), custom_call_target="tpu_custom_call" | custom-call | tf_op jit(solution)/shard_map/pallas_call | solution.py:439
Async XLA Ops:
  2.0 18.1 %all-to-all-start = ((bf16[32,32,128]{2,1,0:T(8,128)(2,1)}), bf16[32,32,128]{2,1,0:T(8,128)(2,1)}, u32[]{:S(2)}, u32[]{:S(2)}) async-start(bf16[32,32,128]{2,1,0:T(8,128)(2,1)} %shard_map.82), calls=%async_computation | async-start | bytes 524288 | tf_op jit(solution)/shard_map/all_to_all | solution.py:393

commit v3 on v2

--- a/solution.py
+++ b/solution.py
@@ -18,9 +18,11 @@
 WIDE = SLAB + 2 * REACH
 NZ = 32
 NY = 32
-GROUPS = (10, 9, 8, 6, 2)
-TAPS = (2, 2, 3, 3)
-STEP = (1, 1, 1, 2)
+GROUPS = (10, 5, 4, 3, 1)
+PHASES = (1, 2, 2, 2, 2)
+TAPS = (2, 2, 2, 3)
+COLSTEP = (1, 1, 2, 4)
+PACKED = 2
 ORIGIN = (-15, -14, -12, -8, 0)
 BF = jnp.bfloat16
 F32 = jnp.float32
@@ -64,20 +66,29 @@
                     block = jnp.where(lane == 0, turned[9 * c + a + 3 * s], 0.0)
                     block = block + pltpu.roll(block, 2 * C, 1)
                     taps[c].append(block + pltpu.roll(block, C, 1))
+            def place(i, t, xi, b, block):
+                lanes = slice(4 * C * b, 4 * C * (b + 1))
+                if layer >= PACKED:
+                    out[s, i, t, xi * C : (xi + 1) * C, lanes] = block
+                elif i == 0:
+                    out[s, t, xi * C : (xi + 1) * C, lanes] = block
+                else:
+                    first = 2 * C * (t % 2) + xi * C
+                    out[s, 4 + t // 2, first : first + C, lanes] = block
+
             for i in range(TAPS[layer]):
-                for xi in range(4):
-                    rows = pl.ds(xi * C, C)
+                for xi in range(4 if i == 0 or layer >= PACKED else 2):
                     for c in range(3):
                         block = jnp.zeros((C, 4 * C), F32)
                         for a in range(3):
-                            xo = 4 * STEP[layer] * i + xi - spacing * a
+                            xo = 4 * i + xi - COLSTEP[layer] * a
                             if 0 <= xo < 4:
                                 block = jnp.where(lane == xo, taps[c][a], block)
                         block = block.astype(BF)
-                        out[s, i, c, rows, 0 : 4 * C] = block
-                        out[s, i, c + 1, rows, 4 * C : 8 * C] = block
-                    out[s, i, 0, rows, 4 * C : 8 * C] = zero
-                    out[s, i, 3, rows, 0 : 4 * C] = zero
+                        for b in range(2):
+                            place(i, c + b, xi, b, block)
+                    place(i, 0, xi, 1, zero)
+                    place(i, 3, xi, 0, zero)
             return carry
 
         lax.fori_loop(0, 3, per_row_tap, 0)
@@ -170,8 +181,18 @@
     return jnp.where(keep, moved, 0.0)
 
 
+def weight_shape(layer):
+    return (3, 6, 4 * C, 8 * C) if layer < PACKED else (3, TAPS[layer], 4, 4 * C, 8 * C)
+
+
 def act_shape(layer):
-    return (3, GROUPS[layer], 2, 2**layer, NZ // 2 ** (layer + 1) + 2, NY, 4 * C)
+    planes = NZ // 2 ** (layer + 1) + 2
+    return (3, PHASES[layer], GROUPS[layer], 2, 2**layer, planes, NY, 4 * C)
+
+
+def edge_shape(layer):
+    planes = NZ // 2 ** (layer + 1) + 1
+    return (3, PHASES[layer], GROUPS[layer] - 1, 2**layer, planes, NY, 4 * C)
 
 
 def act_rows(layer):
@@ -180,7 +201,8 @@
 
 def conv_kernel(off_ref, ramp_ref, pieces_ref, rows_ref, *refs):
     built, out_ref, refs = refs[:5], refs[5], refs[6:]
-    held, stem_in, spaces, accs, sems = refs[:5], refs[5], refs[6:8], refs[8:10], refs[10]
+    held, stem_in, spaces, accs = refs[:5], refs[5], refs[6:8], refs[8:10]
+    sems, edges = refs[10], refs[11:]
     fetches = [
         pltpu.make_async_copy(a, b, sems.at[k]) for k, (a, b) in enumerate(zip(built, held))
     ]
@@ -196,34 +218,46 @@
     first_col = lax.axis_index("gx") * BX + slab * SLAB
     total_cols = lax.axis_size("gx") * BX
 
-    def col_mask(layer, group, width):
+    def col_mask(start, step, width):
         lane = lax.broadcasted_iota(jnp.int32, (1, width * C), 1) // C
-        col = lane + (4 * group + first_col + ORIGIN[layer])
+        col = step * lane + (first_col + start)
         return jnp.where((col >= 0) & (col < total_cols), 1.0, 0.0)
 
     def clear_edges(layer):
         spacing = 2**layer
         pad = jnp.zeros((3, spacing, NY, 4 * C), BF)
-        for g in range(GROUPS[layer]):
-            acts[layer][:, g, 1, :, 0] = pad
-            acts[layer][:, g, 0, :, NZ // (2 * spacing) + 1] = pad
-
-    def store(layer, group, start, length, value):
-        spacing = 2**layer
+        for phase in range(PHASES[layer]):
+            for g in range(GROUPS[layer]):
+                acts[layer][:, phase, g, 1, :, 0] = pad
+                acts[layer][:, phase, g, 0, :, NZ // (2 * spacing) + 1] = pad
+
+    def store(layer, phase, group, start, length, value):
+        spacing = 2**layer
+        rows = slice(start, start + length)
         for s in range(3):
             part = value if s == 1 else shifted(value, spacing if s == 0 else -spacing)
             planes = part.astype(BF).reshape(length, -1, 2, NY, 4 * C)
-            for b in range(2):
-                acts[layer][s, group, b, start : start + length, 1 : 1 + planes.shape[1]] = planes[
-                    :, :, b
-                ]
-
-    def store_plane(layer, group, start, length, m, value):
+            count = planes.shape[1]
+            low, high = planes[:, :, 0], planes[:, :, 1]
+            acts[layer][s, phase, group, 0, rows, 1 : 1 + count] = low
+            acts[layer][s, phase, group, 1, rows, 1 : 1 + count] = high
+            if layer < PACKED and group > 0:
+                low, high = low[..., : 2 * C], high[..., : 2 * C]
+                blank = jnp.zeros((length, 1, NY, 2 * C), BF)
+                out = edges[layer]
+                first = jnp.concatenate([blank, low[:, :1]], axis=-1)
+                inner = jnp.concatenate([high[:, :-1], low[:, 1:]], axis=-1)
+                last = jnp.concatenate([high[:, -1:], blank], axis=-1)
+                out[s, phase, group - 1, rows, 0:1] = first
+                out[s, phase, group - 1, rows, 1:count] = inner
+                out[s, phase, group - 1, rows, count : count + 1] = last
+
+    def store_plane(layer, phase, group, start, length, m, value):
         spacing = 2**layer
         for s in range(3):
             part = value if s == 1 else shifted(value, spacing if s == 0 else -spacing)
             planes = part.astype(BF).reshape(length, NY, 4 * C)
-            acts[layer][s, group, m % 2, start : start + length, 1 + m // 2] = planes
+            acts[layer][s, phase, group, m % 2, start : start + length, 1 + m // 2] = planes
 
     clear_edges(0)
     image = blended_slab(
@@ -248,41 +282,80 @@
         return jnp.dot(lhs, weights, preferred_element_type=F32)
 
     def stem_finish(k, acc):
-        value = jnp.maximum(acc + rows_ref[0:1], 0.0) * col_mask(0, 2 * k, 8)
-        store(0, 2 * k, 0, 1, value[:, : 4 * C])
-        store(0, 2 * k + 1, 0, 1, value[:, 4 * C :])
-
-    def group_dot(layer, g):
+        mask = col_mask(8 * k + ORIGIN[0], 1, 8)
+        value = jnp.maximum(acc + rows_ref[0:1], 0.0) * mask
+        store(0, 0, 2 * k, 0, 1, value[:, : 4 * C])
+        store(0, 0, 2 * k + 1, 0, 1, value[:, 4 * C :])
+
+    def group_dot(layer, phase, g):
         spacing = 2**layer
         count = NZ // (2 * spacing)
+        rows = NZ * NY // 2
         pieces = []
         for s in range(3):
-            for i in range(TAPS[layer]):
-                for t in range(4):
-                    start = (t + 1) // 2
-                    piece = acts[layer][s, g + i, 1 - t % 2, :, start : start + count]
-                    pieces.append(piece.reshape(NZ * NY // 2, 4 * C))
+            for t in range(4):
+                start = (t + 1) // 2
+                piece = acts[layer][s, phase, g, 1 - t % 2, :, start : start + count]
+                pieces.append(piece.reshape(rows, 4 * C))
+            for start in range(2):
+                piece = edges[layer][s, phase, g, :, start : start + count]
+                pieces.append(piece.reshape(rows, 4 * C))
         lhs = jnp.concatenate(pieces, axis=1)
-        weights = w_refs[layer][...].reshape(12 * TAPS[layer] * 4 * C, 8 * C)
+        weights = w_refs[layer][...].reshape(18 * 4 * C, 8 * C)
         return jnp.dot(lhs, weights, preferred_element_type=F32)
 
-    def group_finish(layer, g, acc):
-        spacing = 2**layer
-        count = NZ // (2 * spacing)
-        mask = col_mask(layer + 1, g, 4)
+    def centred(layer, phase, g, b, planes, rows):
+        near = [acts[layer][1, phase, g + i, b, :, planes].reshape(rows, 4 * C) for i in range(2)]
+        pair = jnp.concatenate(near, axis=1).astype(F32)
+        first = COLSTEP[layer] * C
+        return pair[:, first : first + 4 * C]
+
+    def group_values(layer, phase, g, acc, mask):
+        count = NZ // (2 * 2**layer)
         bias = rows_ref[8 + layer : 9 + layer, : 4 * C]
+        values = []
         for b in range(2):
-            pair = jnp.concatenate(
-                [
-                    acts[layer][1, g + i, b, :, 1 : 1 + count].reshape(NZ * NY // 2, 4 * C)
-                    for i in range(2)
-                ],
-                axis=1,
-            ).astype(F32)
-            centre = pair[:, spacing * C : spacing * C + 4 * C]
-            half = acc[0 : NZ * NY // 2, 4 * C * b : 4 * C * (b + 1)] + bias
-            value = centre + jnp.maximum(half, 0.0) * mask
-            store(layer + 1, g, spacing * b, spacing, value)
+            centre = centred(layer, phase, g, b, slice(1, 1 + count), NZ * NY // 2)
+            half = acc[:, 4 * C * b : 4 * C * (b + 1)] + bias
+            values.append(centre + jnp.maximum(half, 0.0) * mask)
+        return values
+
+    def split_store(k, left, right):
+        for b in range(2):
+            one = left[b]
+            block = lax.broadcasted_iota(jnp.int32, one.shape, 1) // C
+            up, far = pltpu.roll(one, 3 * C, 1), pltpu.roll(one, 2 * C, 1)
+            even = jnp.where(block == 0, one, up)
+            odd = jnp.where(block == 0, up, far)
+            if right is None:
+                even_end = odd_end = jnp.zeros_like(one)
+            else:
+                two = right[b]
+                down, far = pltpu.roll(two, C, 1), pltpu.roll(two, 2 * C, 1)
+                even_end = jnp.where(block == 2, far, down)
+                odd_end = jnp.where(block == 2, down, two)
+            store(1, 0, k, b, 1, jnp.where(block < 2, even, even_end))
+            store(1, 1, k, b, 1, jnp.where(block < 2, odd, odd_end))
+
+    def first_layer():
+        left = None
+        for g in range(GROUPS[0] - 1):
+            mask = col_mask(4 * g + ORIGIN[1], 1, 4)
+            values = group_values(0, 0, g, group_dot(0, 0, g), mask)
+            if left is None:
+                left = values
+            else:
+                split_store(g // 2, left, values)
+                left = None
+        split_store(GROUPS[1] - 1, left, None)
+
+    def second_layer():
+        for phase in range(2):
+            for g in range(GROUPS[2]):
+                mask = col_mask(8 * g + phase + ORIGIN[2], 2, 4)
+                values = group_values(1, phase, g, group_dot(1, phase, g), mask)
+                for b in range(2):
+                    store(2, phase, g, 2 * b, 2, values[b])
 
     def plane_dot(layer, m):
         spacing = 2**layer
@@ -292,9 +365,8 @@
         for s in range(3):
             for i in range(TAPS[layer]):
                 for t in taps:
-                    first = STEP[layer] * i
-                    piece = acts[layer][s, first : first + groups, 1 - t % 2, :, m + (t + 1) // 2]
-                    pieces.append(piece.reshape(groups * spacing * NY, 4 * C))
+                    piece = acts[layer][s, :, i : i + groups, 1 - t % 2, :, m + (t + 1) // 2]
+                    pieces.append(piece.reshape(2 * groups * spacing * NY, 4 * C))
                     weights.append(w_refs[layer][s, i, t])
         return jnp.dot(
             jnp.concatenate(pieces, axis=1),
@@ -302,29 +374,34 @@
             preferred_element_type=F32,
         )
 
-    def plane_values(layer, m, g, acc):
+    def plane_values(layer, m, phase, g, acc):
         spacing = 2**layer
         rows = spacing * NY
-        mask = col_mask(layer + 1, g, 4)
+        mask = col_mask(8 * g + phase + ORIGIN[layer + 1], 2, 4)
         bias = rows_ref[8 + layer : 9 + layer, : 4 * C]
+        at = (phase * GROUPS[layer + 1] + g) * rows
         values = []
         for b in range(2):
-            centre = acts[layer][1, g + STEP[layer], b, :, 1 + m].reshape(rows, 4 * C)
-            half = acc[g * rows : (g + 1) * rows, 4 * C * b : 4 * C * (b + 1)] + bias
-            values.append(centre.astype(F32) + jnp.maximum(half, 0.0) * mask)
+            if COLSTEP[layer] < 4:
+                centre = centred(layer, phase, g, b, 1 + m, rows)
+            else:
+                centre = acts[layer][1, phase, g + 1, b, :, 1 + m].reshape(rows, 4 * C).astype(F32)
+            half = acc[at : at + rows, 4 * C * b : 4 * C * (b + 1)] + bias
+            values.append(centre + jnp.maximum(half, 0.0) * mask)
         return values
 
     def plane_finish(layer, m, acc):
         spacing = 2**layer
-        for g in range(GROUPS[layer + 1]):
-            for b, value in enumerate(plane_values(layer, m, g, acc)):
-                store_plane(layer + 1, g, spacing * b, spacing, m, value)
+        for phase in range(2):
+            for g in range(GROUPS[layer + 1]):
+                for b, value in enumerate(plane_values(layer, m, phase, g, acc)):
+                    store_plane(layer + 1, phase, g, spacing * b, spacing, m, value)
 
     def head_finish(m, acc):
         layer = LAYERS - 1
         spacing = 2**layer
-        for g in range(GROUPS[layer + 1]):
-            last = jnp.concatenate(plane_values(layer, m, g, acc), axis=1)
+        for phase in range(2):
+            last = jnp.concatenate(plane_values(layer, m, phase, 0, acc), axis=1)
             last = last.reshape(spacing, row_parts, NY // row_parts, 8 * C)
             last = last.transpose(1, 0, 2, 3).reshape(spacing * NY, 8 * C).astype(BF)
             heads = lax.dot_general(
@@ -336,9 +413,10 @@
             size = spacing * NY // row_parts
             for y in range(row_parts):
                 for b in range(2):
-                    out_ref[(2 * m + b) * row_parts + y, 4 * g : 4 * g + 4, 0:size] = heads[
-                        4 * b : 4 * b + 4, y * size : (y + 1) * size
-                    ]
+                    for x in range(4):
+                        out_ref[
+                            (2 * m + b) * row_parts + y, 2 * x + phase : 2 * x + phase + 1, 0:size
+                        ] = heads[4 * b + x : 4 * b + x + 1, y * size : (y + 1) * size]
 
     def in_line(count, dot, finish):
         for k in range(count):
@@ -350,13 +428,11 @@
         fetches[1 + layer].wait()
         if layer + 1 < LAYERS:
             clear_edges(layer + 1)
-        if layer < 2:
-            in_line(
-                GROUPS[layer + 1],
-                functools.partial(group_dot, layer),
-                functools.partial(group_finish, layer),
-            )
-        elif layer + 1 < LAYERS:
+        if layer == 0:
+            first_layer()
+        elif layer == 1:
+            second_layer()
+        elif layer == 2:
             in_line(
                 NZ // 2 ** (layer + 1),
                 functools.partial(plane_dot, layer),
@@ -396,7 +472,7 @@
     hbm = pl.BlockSpec(memory_space=pltpu.HBM)
     small = jax.ShapeDtypeStruct((24, 8 * C), F32)
     shapes = [jax.ShapeDtypeStruct((GROUPS[0] // 2, 384, 8 * C), BF)] + [
-        jax.ShapeDtypeStruct((3, TAPS[layer], 4, 4 * C, 8 * C), BF) for layer in range(LAYERS)
+        jax.ShapeDtypeStruct(weight_shape(layer), BF) for layer in range(LAYERS)
     ]
     spaces = [pltpu.VMEM(shape.shape, shape.dtype) for shape in shapes]
     raw = (layer_weight, layer_bias, stem_weight, stem_bias[None], head_weight[None])
@@ -423,6 +499,7 @@
         + [pltpu.VMEM((size, NY, 4 * C), BF) for size in held]
         + [pltpu.VMEM((NZ * NY // 2, 8 * C), F32)] * 2
         + [pltpu.SemaphoreType.DMA((5,))]
+        + [pltpu.VMEM(edge_shape(layer), BF) for layer in range(PACKED)]
     )
     logits = pl.pallas_call(
         conv_kernel,

time: 64.9 us -> 61.1 us (0.941)
  Pallas kernels: 43.1 us -> 39.2 us
    pallas_call x1, Pallas kernels: 31.8 us -> 28 us  [body(): pl.pallas_call(conv_kernel, out_shape=jax.ShapeDtypeStruct((parts, SLAB,...]
  transfers between devices with their start and end apart: 1 -> 1, of which waited for: 1 -> 1; matrix products, arithmetic and copies ran while one was open for 0% -> 0% of each run, Pallas kernels for 12% -> 13%
where the time goes in v3:
time: 61.1 us; the launch traced here: 60.7 us
  Pallas kernels  39.2 us (64%)
  blocking collectives  11 us (18%)
  starting transfers between devices  7.43 us (12%)
  waiting for transfers between devices  3.01 us (5%)
    pallas_call x1, Pallas kernels, body(): pl.pallas_call(conv_kernel, out_shape=jax.ShapeDtypeStruct((parts, SLAB,...  28 us
    all_to_all x1, blocking collectives, body(): logits = lax.all_to_all(logits, ('gz', 'gy'), 0, 0, tiled=True)  11 us
    pallas_call x1, Pallas kernels, body(): pl.pallas_call(weights_kernel, out_shape=[small] + shapes, in_specs=[hbm]...  7.65 us
    all_to_all x1, starting transfers between devices, body(): pieces = lax.all_to_all(pieces, ('gz', 'gy', 'gx'), 0, 0, tiled=True)  7.43 us
    all_to_all x1, waiting for transfers between devices, body(): pieces = lax.all_to_all(pieces, ('gz', 'gy', 'gx'), 0, 0, tiled=True)  3.01 us
    pallas_call x1, Pallas kernels, body(): pl.pallas_call(functools.partial(pack_kernel, parts=parts, bricks=bricks)...  1.96 us
    pallas_call x1, Pallas kernels, body(): pl.pallas_call(unpack_kernel, out_shape=jax.ShapeDtypeStruct((depth_b * r...  1.54 us
  transfers between devices with their start and end apart: 1, of which 1 were waited for; matrix products, arithmetic and copies ran while one was open for 0% of the time, Pallas kernels for 13%

profile of v3, /device:TPU:0, one launch (start us, length us, event | category | flops | bytes accessed | tf_op | source)
XLA Modules:
  0.0 60.7 jit_solution(6825714599603949888)
XLA Ops:
  0.0 2.0 %shard_map.82 = bf16[32,32,128]{2,1,0:T(8,128)(2,1)} custom-call(s32[2]{0:T(128)} %off_ref.3, bf16[8,8,256]{2,1,0:T(8,128)(2,1)} %stacks_ref.1), custom_call_target="tpu_custom_call" | custom-call | tf_op jit(solution)/shard_map/pallas_call | solution.py:463
  2.0 7.4 %all-to-all-start = ((bf16[32,32,128]{2,1,0:T(8,128)(2,1)}), bf16[32,32,128]{2,1,0:T(8,128)(2,1)}, u32[]{:S(2)}, u32[]{:S(2)}) async-start(bf16[32,32,128]{2,1,0:T(8,128)(2,1)} %shard_map.82), calls=%async_computation | async-start | bytes 524288 | tf_op jit(solution)/shard_map/all_to_all | solution.py:469
  9.4 7.7 %shard_map.83 = (f32[24,256]{1,0:T(8,128)}, bf16[5,384,256]{2,1,0:T(8,128)(2,1)}, bf16[3,6,128,256]{3,2,1,0:T(8,128)(2,1)}, bf16[3,6,128,256]{3,2,1,0:T(8,128)(2...) custom-call(bf16[4,27,32,32]{3,2,1,0:T(8,128)(2,1)} %refs_0_.1, f32[4,32]{1,0:T(4,128)} %refs_1_.1, ...), custom_call_target="tpu_custom_call" | custom-call | flops 4000000 | bytes 9000000 | tf_op jit(solution)/shard_map/pallas_call | solution.py:479
  17.1 3.0 %all-to-all-done = bf16[32,32,128]{2,1,0:T(8,128)(2,1)} async-done(((bf16[32,32,128]{2,1,0:T(8,128)(2,1)}), bf16[32,32,128]{2,1,0:T(8,128)(2,1)}, u32[]{:S(2)}, u32[]{:S(2)}) %all-to-all-start) | async-done | bytes 262176 | tf_op jit(solution)/shard_map/all_to_all | solution.py:469
  20.1 28.0 %shard_map.84 = f32[16,8,128]{2,1,0:T(8,128)} custom-call(s32[2]{0:T(128)} %off_ref.3, s32[2]{0:T(128)} %ramp_ref.1, bf16[4,4,2,32,128]{4,3,2,1,0:T(8,128)(2,1)} %bitcast.pieces_ref, f32[24,256]{1,0:T(8,128)} %get-tuple-element.11.rows_ref, bf16[5,384,256]{2,1,0:T(8,128)(2,1)} %get-tuple-element.12.refs_0_, ...), custom_call_target="tpu_custom_call" | custom-call | flops 20000000000 | bytes 9000000 | tf_op jit(solution)/shard_map/pallas_call | solution.py:504
  48.1 11.0 %all_to_all.10.pieces_ref = f32[16,8,128]{2,1,0:T(8,128)} all-to-all(f32[16,8,128]{2,1,0:T(8,128)} %shard_map.84), channel_id=1, replica_groups=mesh['gz'=4,'gy'=4,'gx'=2] {'gz','gy'}, dimensions={0} | all-to-all | bytes 131072 | tf_op jit(solution)/shard_map/all_to_all | solution.py:515
  59.2 1.5 %shard_map.85 = f32[64,128]{1,0:T(8,128)} custom-call(f32[16,8,128]{2,1,0:T(8,128)} %all_to_all.10.pieces_ref), custom_call_target="tpu_custom_call" | custom-call | tf_op jit(solution)/shard_map/pallas_call | solution.py:516
Async XLA Ops:
  2.0 18.1 %all-to-all-start = ((bf16[32,32,128]{2,1,0:T(8,128)(2,1)}), bf16[32,32,128]{2,1,0:T(8,128)(2,1)}, u32[]{:S(2)}, u32[]{:S(2)}) async-start(bf16[32,32,128]{2,1,0:T(8,128)(2,1)} %shard_map.82), calls=%async_computation | async-start | bytes 524288 | tf_op jit(solution)/shard_map/all_to_all | solution.py:469

commit v4 on v3

--- a/solution.py
+++ b/solution.py
@@ -134,10 +134,6 @@
             low = pltpu.roll(moved[:rows], (tile_len - SLAB * j) % tile_len, 1)[:, :128]
             high = pltpu.roll(moved[rows:], (tile_len + 64 - SLAB * j) % tile_len, 1)[:, :128]
             out_ref[j * bricks + other] = jnp.where(lane < 64, low, high).astype(BF)
-
-
-def unpack_kernel(pieces_ref, out_ref):
-    out_ref[...] = pieces_ref[...].reshape(128, 128).T[: out_ref.shape[0]]
 
 
 def blended_slab(off_ref, ramp_ref, pieces_ref, first_col, total_cols, depth_parts, row_parts):
@@ -174,11 +170,13 @@
 
 
 def shifted(value, by):
-    rows = value.shape[0]
-    spot = lax.broadcasted_iota(jnp.int32, value.shape, 0) % NY
-    moved = pltpu.roll(value, by % rows, 0)
-    keep = (spot >= by) if by > 0 else (spot < NY + by)
-    return jnp.where(keep, moved, 0.0)
+    planes = value.reshape(-1, NY, value.shape[1])
+    blank = jnp.zeros((planes.shape[0], abs(by), value.shape[1]), value.dtype)
+    if by > 0:
+        moved = jnp.concatenate([blank, planes[:, : NY - by]], axis=1)
+    else:
+        moved = jnp.concatenate([planes[:, -by:], blank], axis=1)
+    return moved.reshape(value.shape)
 
 
 def weight_shape(layer):
@@ -260,6 +258,7 @@
             acts[layer][s, phase, group, m % 2, start : start + length, 1 + m // 2] = planes
 
     clear_edges(0)
+    clear_edges(1)
     image = blended_slab(
         off_ref, ramp_ref, pieces_ref, first_col, total_cols, depth_parts, row_parts
     )
@@ -306,9 +305,9 @@
 
     def centred(layer, phase, g, b, planes, rows):
         near = [acts[layer][1, phase, g + i, b, :, planes].reshape(rows, 4 * C) for i in range(2)]
-        pair = jnp.concatenate(near, axis=1).astype(F32)
+        pair = jnp.concatenate(near, axis=1)
         first = COLSTEP[layer] * C
-        return pair[:, first : first + 4 * C]
+        return pair[:, first : first + 4 * C].astype(F32)
 
     def group_values(layer, phase, g, acc, mask):
         count = NZ // (2 * 2**layer)
@@ -350,12 +349,13 @@
         split_store(GROUPS[1] - 1, left, None)
 
     def second_layer():
-        for phase in range(2):
-            for g in range(GROUPS[2]):
-                mask = col_mask(8 * g + phase + ORIGIN[2], 2, 4)
-                values = group_values(1, phase, g, group_dot(1, phase, g), mask)
-                for b in range(2):
-                    store(2, phase, g, 2 * b, 2, values[b])
+        order = [(phase, g) for phase in range(2) for g in range(GROUPS[2])]
+        order.sort(key=lambda pair: pair[1] == GROUPS[2] - 1)
+        for phase, g in order:
+            mask = col_mask(8 * g + phase + ORIGIN[2], 2, 4)
+            values = group_values(1, phase, g, group_dot(1, phase, g), mask)
+            for b in range(2):
+                store(2, phase, g, 2 * b, 2, values[b])
 
     def plane_dot(layer, m):
         spacing = 2**layer
@@ -423,11 +423,12 @@
             finish(k, dot(k))
 
     fetches[0].wait()
-    in_line(GROUPS[0] // 2, stem_dot, stem_finish)
+    for k in range(GROUPS[0] // 2):
+        if k == GROUPS[0] // 2 - 1:
+            for copy in fetches[1:]:
+                copy.wait()
+        stem_finish(k, stem_dot(k))
     for layer in range(LAYERS):
-        fetches[1 + layer].wait()
-        if layer + 1 < LAYERS:
-            clear_edges(layer + 1)
         if layer == 0:
             first_layer()
         elif layer == 1:
@@ -513,12 +514,7 @@
         ),
     )(offsets, ramp_width, pieces, rows, *weights)
     logits = lax.all_to_all(logits, ("gz", "gy"), 0, 0, tiled=True)
-    logits = pl.pallas_call(
-        unpack_kernel,
-        out_shape=jax.ShapeDtypeStruct((depth_b * rows_b, BX), F32),
-        in_specs=[vmem()],
-        out_specs=vmem(),
-    )(logits)
+    logits = logits[:, :, : depth_b * rows_b].transpose(2, 0, 1)
     return logits.reshape(depth_b, rows_b, BX)
 
 

time: 61.1 us -> 56.7 us (0.928)
  Pallas kernels: 39.2 us -> 34.5 us
  local copies, waits for them, and re-layouts: 0 us -> 1.01 us
  blocking collectives: 11 us -> 10.3 us
    pallas_call x1, Pallas kernels: 28 us -> 24.9 us  [body(): pl.pallas_call(conv_kernel, out_shape=jax.ShapeDtypeStruct((parts, SLAB,...]
    pallas_call x1 -> x0, Pallas kernels: 1.54 us -> none  [body(): pl.pallas_call(unpack_kernel, out_shape=jax.ShapeDtypeStruct((depth_b * r...]
    reshape x0 -> x2, local copies, waits for them, and re-layouts: none -> 1 us  [body(): return logits.reshape(depth_b, rows_b, BX)]
    all_to_all x1, blocking collectives: 11 us -> 10.3 us  [body(): logits = lax.all_to_all(logits, ('gz', 'gy'), 0, 0, tiled=True)]
  transfers between devices with their start and end apart: 1 -> 1, of which waited for: 1 -> 1; matrix products, arithmetic and copies ran while one was open for 0% -> 0% of each run, Pallas kernels for 13% -> 14%
where the time goes in v4:
time: 56.7 us; the launch traced here: 56.3 us
  Pallas kernels  34.5 us (61%)
  blocking collectives  10.3 us (18%)
  starting transfers between devices  7.43 us (13%)
  waiting for transfers between devices  3.01 us (5%)
  local copies, waits for them, and re-layouts  1.01 us (2%)
    pallas_call x1, Pallas kernels, body(): pl.pallas_call(conv_kernel, out_shape=jax.ShapeDtypeStruct((parts, SLAB,...  24.9 us
    all_to_all x1, blocking collectives, body(): logits = lax.all_to_all(logits, ('gz', 'gy'), 0, 0, tiled=True)  10.3 us
    pallas_call x1, Pallas kernels, body(): pl.pallas_call(weights_kernel, out_shape=[small] + shapes, in_specs=[hbm]...  7.65 us
    all_to_all x1, starting transfers between devices, body(): pieces = lax.all_to_all(pieces, ('gz', 'gy', 'gx'), 0, 0, tiled=True)  7.43 us
    all_to_all x1, waiting for transfers between devices, body(): pieces = lax.all_to_all(pieces, ('gz', 'gy', 'gx'), 0, 0, tiled=True)  3.01 us
    pallas_call x1, Pallas kernels, body(): pl.pallas_call(functools.partial(pack_kernel, parts=parts, bricks=bricks)...  1.96 us
  transfers between devices with their start and end apart: 1, of which 1 were waited for; matrix products, arithmetic and copies ran while one was open for 0% of the time, Pallas kernels for 14%

profile of v4, /device:TPU:0, one launch (start us, length us, event | category | flops | bytes accessed | tf_op | source)
XLA Modules:
  0.0 56.3 jit_solution(5479332213926589651)
XLA Ops:
  0.0 2.0 %shard_map.82 = bf16[32,32,128]{2,1,0:T(8,128)(2,1)} custom-call(s32[2]{0:T(128)} %off_ref.3, bf16[8,8,256]{2,1,0:T(8,128)(2,1)} %stacks_ref.1), custom_call_target="tpu_custom_call" | custom-call | tf_op jit(solution)/shard_map/pallas_call | solution.py:464
  2.0 7.4 %all-to-all-start = ((bf16[32,32,128]{2,1,0:T(8,128)(2,1)}), bf16[32,32,128]{2,1,0:T(8,128)(2,1)}, u32[]{:S(2)}, u32[]{:S(2)}) async-start(bf16[32,32,128]{2,1,0:T(8,128)(2,1)} %shard_map.82), calls=%async_computation | async-start | bytes 524288 | tf_op jit(solution)/shard_map/all_to_all | solution.py:470
  9.4 7.7 %shard_map.83 = (f32[24,256]{1,0:T(8,128)}, bf16[5,384,256]{2,1,0:T(8,128)(2,1)}, bf16[3,6,128,256]{3,2,1,0:T(8,128)(2,1)}, bf16[3,6,128,256]{3,2,1,0:T(8,128)(2...) custom-call(bf16[4,27,32,32]{3,2,1,0:T(8,128)(2,1)} %refs_0_.1, f32[4,32]{1,0:T(4,128)} %refs_1_.1, ...), custom_call_target="tpu_custom_call" | custom-call | flops 4000000 | bytes 9000000 | tf_op jit(solution)/shard_map/pallas_call | solution.py:480
  17.1 3.0 %all-to-all-done = bf16[32,32,128]{2,1,0:T(8,128)(2,1)} async-done(((bf16[32,32,128]{2,1,0:T(8,128)(2,1)}), bf16[32,32,128]{2,1,0:T(8,128)(2,1)}, u32[]{:S(2)}, u32[]{:S(2)}) %all-to-all-start) | async-done | bytes 262176 | tf_op jit(solution)/shard_map/all_to_all | solution.py:470
  20.1 24.9 %shard_map.84 = f32[16,8,128]{2,1,0:T(8,128)} custom-call(s32[2]{0:T(128)} %off_ref.3, s32[2]{0:T(128)} %ramp_ref.1, bf16[4,4,2,32,128]{4,3,2,1,0:T(8,128)(2,1)} %bitcast.pieces_ref, f32[24,256]{1,0:T(8,128)} %get-tuple-element.11.rows_ref, bf16[5,384,256]{2,1,0:T(8,128)(2,1)} %get-tuple-element.12.refs_0_, ...), custom_call_target="tpu_custom_call" | custom-call | flops 20000000000 | bytes 9000000 | tf_op jit(solution)/shard_map/pallas_call | solution.py:505
  44.9 10.3 %all_to_all.10 = f32[16,8,128]{2,1,0:T(8,128)S(1)} all-to-all(f32[16,8,128]{2,1,0:T(8,128)} %shard_map.84), channel_id=1, replica_groups=mesh['gz'=4,'gy'=4,'gx'=2] {'gz','gy'}, dimensions={0} | all-to-all | bytes 131072 | tf_op jit(solution)/shard_map/all_to_all | solution.py:516
  55.3 0.2 reshape.8
  55.5 0.8 %copy.11 = f32[8,8,128]{2,1,0:T(8,128)} copy(f32[8,8,128]{1,0,2:T(8,128)S(1)} %reshape.8) | data formatting | bytes 65536 | tf_op jit(solution)/shard_map/reshape | solution.py:518
  (1 shorter events, 0.0 us)
Async XLA Ops:
  2.0 18.1 %all-to-all-start = ((bf16[32,32,128]{2,1,0:T(8,128)(2,1)}), bf16[32,32,128]{2,1,0:T(8,128)(2,1)}, u32[]{:S(2)}, u32[]{:S(2)}) async-start(bf16[32,32,128]{2,1,0:T(8,128)(2,1)} %shard_map.82), calls=%async_computation | async-start | bytes 524288 | tf_op jit(solution)/shard_map/all_to_all | solution.py:470

commit v5 on v4

--- a/solution.py
+++ b/solution.py
@@ -17,6 +17,7 @@
 SLAB = 8
 WIDE = SLAB + 2 * REACH
 NZ = 32
+DEPTHS = (0, 3, 5)
 NY = 32
 GROUPS = (10, 5, 4, 3, 1)
 PHASES = (1, 2, 2, 2, 2)
@@ -123,48 +124,58 @@
 
 def pack_kernel(off_ref, stacks_ref, out_ref, *, parts, bricks):
     brick = lax.axis_index("gx")
-    tile_len = stacks_ref.shape[2]
-    rows = out_ref.shape[1]
-    values = stacks_ref[...].astype(F32).reshape(2 * rows, tile_len)
+    depth, height, tile_len = stacks_ref.shape
+    rows = 3 * height
+    values = stacks_ref[...].astype(F32).reshape(depth * height, tile_len)
     lane = lax.broadcasted_iota(jnp.int32, (rows, 128), 1)
+    turned = []
     for other in range(bricks):
         first = other * BX - REACH - (brick * BX - H + off_ref[brick])
-        moved = pltpu.roll(values, lax.rem(64 * tile_len - first, tile_len), 1)
-        for j in range(parts):
-            low = pltpu.roll(moved[:rows], (tile_len - SLAB * j) % tile_len, 1)[:, :128]
-            high = pltpu.roll(moved[rows:], (tile_len + 64 - SLAB * j) % tile_len, 1)[:, :128]
-            out_ref[j * bricks + other] = jnp.where(lane < 64, low, high).astype(BF)
+        turned.append(pltpu.roll(values, lax.rem(64 * tile_len - first, tile_len), 1))
+    for j in range(parts):
+        messages = []
+        for moved in turned:
+            blocks = []
+            for k, z in enumerate(DEPTHS):
+                block = moved[z * height : z * height + rows]
+                by = (tile_len + WIDE * k - SLAB * j) % tile_len
+                blocks.append(pltpu.roll(block, by, 1)[:, :128])
+            later = jnp.where(lane < 2 * WIDE, blocks[1], blocks[2])
+            messages.append(jnp.where(lane < WIDE, blocks[0], later))
+        message = jnp.concatenate(messages, axis=0).astype(BF)
+        out_ref[j * bricks * rows : (j + 1) * bricks * rows] = message
 
 
 def blended_slab(off_ref, ramp_ref, pieces_ref, first_col, total_cols, depth_parts, row_parts):
     bricks = lax.axis_size("gx")
-    brick = lax.axis_index("gx")
-    lane = lax.broadcasted_iota(jnp.int32, (1, 128), 1) % 64
+    lane = lax.broadcasted_iota(jnp.int32, (1, 128), 1)
+    lane = jnp.where(lane < WIDE, lane, jnp.where(lane < 2 * WIDE, lane - WIDE, lane - 2 * WIDE))
     col = lane + (first_col - REACH)
-    numerator = jnp.zeros((depth_parts, row_parts, 32, 128), F32)
+    height = NY // row_parts
+    pieces = pieces_ref[...].astype(F32)
+    pieces = pieces.reshape(depth_parts, row_parts, bricks, 3 * height, 128)
+    numerator = jnp.zeros((depth_parts, row_parts, 3 * height, 128), F32)
     denominator = jnp.zeros((1, 128), F32)
-    for step in range(min(bricks, 3)):
-        if bricks > 3:
-            tile = jnp.clip(brick - 1 + step, 0, bricks - 1)
-            real = (brick - 1 + step >= 0) & (brick - 1 + step < bricks)
-        else:
-            tile, real = step, True
+    for tile in range(bricks):
         tile_len = 2 * BX
         spot = col - (tile * BX - H + off_ref[tile])
-        inside = (spot >= 0) & (spot < tile_len) & real
+        inside = (spot >= 0) & (spot < tile_len)
         width = ramp_ref[tile].astype(F32)
         spot = spot.astype(F32)
         weight = jnp.minimum(1.0, jnp.minimum((spot + 1.0) / width, (tile_len - spot) / width))
         weight = jnp.where(inside, weight, 0.0)
         denominator = denominator + weight
-        values = pieces_ref[:, :, tile].astype(F32)
-        numerator = numerator + values * weight
+        numerator = numerator + pieces[:, :, tile] * weight
     good = (col >= 0) & (col < total_cols)
     result = jnp.where(good, numerator / jnp.where(good, denominator, 1.0), 0.0)
-    zrows = result.reshape(depth_parts, row_parts, 4, 8, 128)
-    low = zrows.transpose(0, 2, 1, 3, 4)
-    high = pltpu.roll(result.reshape(-1, 128), 64, 1).reshape(zrows.shape).transpose(0, 2, 1, 3, 4)
-    image = jnp.stack([low, high], axis=1).reshape(NZ * NY, 128)
+    blocks = []
+    for k in range(3):
+        block = result.reshape(-1, 128)
+        if k:
+            block = pltpu.roll(block, 128 - WIDE * k, 1)
+        block = block.reshape(depth_parts, row_parts, 3, height, 128)
+        blocks.append(block if k < 2 else block[:, :, 1:])
+    image = jnp.concatenate(blocks, axis=2).transpose(0, 2, 1, 3, 4).reshape(NZ * NY, 128)
     lanes = lax.broadcasted_iota(jnp.int32, image.shape, 1)
     return jnp.where(lanes < WIDE, image, 0.0)
 
@@ -357,15 +368,14 @@
             for b in range(2):
                 store(2, phase, g, 2 * b, 2, values[b])
 
-    def plane_dot(layer, m):
-        spacing = 2**layer
-        groups = GROUPS[layer + 1]
+    def plane_dot(layer, m, first=0, groups=1):
+        spacing = 2**layer
         taps = [t for t in range(4) if 0 < m + (t + 1) // 2 < NZ // (2 * spacing) + 1]
         pieces, weights = [], []
         for s in range(3):
             for i in range(TAPS[layer]):
                 for t in taps:
-                    piece = acts[layer][s, :, i : i + groups, 1 - t % 2, :, m + (t + 1) // 2]
+                    piece = acts[layer][s, :, i + first : i + first + groups, 1 - t % 2, :, m + (t + 1) // 2]
                     pieces.append(piece.reshape(2 * groups * spacing * NY, 4 * C))
                     weights.append(w_refs[layer][s, i, t])
         return jnp.dot(
@@ -374,12 +384,12 @@
             preferred_element_type=F32,
         )
 
-    def plane_values(layer, m, phase, g, acc):
+    def plane_values(layer, m, phase, g, acc, first=0, groups=1):
         spacing = 2**layer
         rows = spacing * NY
         mask = col_mask(8 * g + phase + ORIGIN[layer + 1], 2, 4)
         bias = rows_ref[8 + layer : 9 + layer, : 4 * C]
-        at = (phase * GROUPS[layer + 1] + g) * rows
+        at = (phase * groups + g - first) * rows
         values = []
         for b in range(2):
             if COLSTEP[layer] < 4:
@@ -390,11 +400,12 @@
             values.append(centre + jnp.maximum(half, 0.0) * mask)
         return values
 
-    def plane_finish(layer, m, acc):
+    def plane_finish(layer, m, first, groups, acc):
         spacing = 2**layer
         for phase in range(2):
-            for g in range(GROUPS[layer + 1]):
-                for b, value in enumerate(plane_values(layer, m, phase, g, acc)):
+            for g in range(first, first + groups):
+                values = plane_values(layer, m, phase, g, acc, first, groups)
+                for b, value in enumerate(values):
                     store_plane(layer + 1, phase, g, spacing * b, spacing, m, value)
 
     def head_finish(m, acc):
@@ -418,10 +429,6 @@
                             (2 * m + b) * row_parts + y, 2 * x + phase : 2 * x + phase + 1, 0:size
                         ] = heads[4 * b + x : 4 * b + x + 1, y * size : (y + 1) * size]
 
-    def in_line(count, dot, finish):
-        for k in range(count):
-            finish(k, dot(k))
-
     fetches[0].wait()
     for k in range(GROUPS[0] // 2):
         if k == GROUPS[0] // 2 - 1:
@@ -434,11 +441,9 @@
         elif layer == 1:
             second_layer()
         elif layer == 2:
-            in_line(
-                NZ // 2 ** (layer + 1),
-                functools.partial(plane_dot, layer),
-                functools.partial(plane_finish, layer),
-            )
+            for first, groups in ((0, GROUPS[3] - 1), (GROUPS[3] - 1, 1)):
+                for m in range(NZ // 2 ** (layer + 1)):
+                    plane_finish(layer, m, first, groups, plane_dot(layer, m, first, groups))
         else:
             for m in range(NZ // 2 ** (layer + 1)):
                 accs[m][...] = plane_dot(layer, m)
@@ -459,16 +464,15 @@
     parts = depth_parts * row_parts
     bricks = lax.axis_size("gx")
     assert (depth_b * depth_parts, rows_b * row_parts, parts * SLAB) == (NZ, NY, BX)
-    half = depth_b * rows_b // 2
+    assert depth_b == DEPTHS[-1] + 3
     smem = pl.BlockSpec(memory_space=pltpu.SMEM)
     pieces = pl.pallas_call(
         functools.partial(pack_kernel, parts=parts, bricks=bricks),
-        out_shape=jax.ShapeDtypeStruct((parts * bricks, half, 128), BF),
+        out_shape=jax.ShapeDtypeStruct((parts * bricks * 3 * rows_b, 128), BF),
         in_specs=[smem, vmem()],
         out_specs=vmem(),
     )(offsets, stacks)
     pieces = lax.all_to_all(pieces, ("gz", "gy", "gx"), 0, 0, tiled=True)
-    pieces = pieces.reshape(depth_parts, row_parts, bricks, half, 128)
 
     hbm = pl.BlockSpec(memory_space=pltpu.HBM)
     small = jax.ShapeDtypeStruct((24, 8 * C), F32)

time: 56.7 us -> 55.5 us (0.979)
  Pallas kernels: 34.5 us -> 33.3 us
  waiting for transfers between devices: 3.01 us -> 1.99 us
  local copies, waits for them, and re-layouts: 1.01 us -> 1.69 us
    pallas_call x1, Pallas kernels: 24.9 us -> 23.8 us  [body(): pl.pallas_call(conv_kernel, out_shape=jax.ShapeDtypeStruct((parts, SLAB,...]
    all_to_all x1, waiting for transfers between devices: 3.01 us -> 1.99 us  [body(): pieces = lax.all_to_all(pieces, ('gz', 'gy', 'gx'), 0, 0, tiled=True)]
    unnamed x0 -> x2, local copies, waits for them, and re-layouts: none -> 0.68 us
where the time goes in v5:
time: 55.5 us; the launch traced here: 55.2 us
  Pallas kernels  33.3 us (60%)
  blocking collectives  10.8 us (19%)
  starting transfers between devices  7.3 us (13%)
  waiting for transfers between devices  1.99 us (4%)
  local copies, waits for them, and re-layouts  1.69 us (3%)
    pallas_call x1, Pallas kernels, body(): pl.pallas_call(conv_kernel, out_shape=jax.ShapeDtypeStruct((parts, SLAB,...  23.8 us
    all_to_all x1, blocking collectives, body(): logits = lax.all_to_all(logits, ('gz', 'gy'), 0, 0, tiled=True)  10.8 us
    pallas_call x1, Pallas kernels, body(): pl.pallas_call(weights_kernel, out_shape=[small] + shapes, in_specs=[hbm]...  7.67 us
    all_to_all x1, starting transfers between devices, body(): pieces = lax.all_to_all(pieces, ('gz', 'gy', 'gx'), 0, 0, tiled=True)  7.3 us
    all_to_all x1, waiting for transfers between devices, body(): pieces = lax.all_to_all(pieces, ('gz', 'gy', 'gx'), 0, 0, tiled=True)  1.99 us
    pallas_call x1, Pallas kernels, body(): pl.pallas_call(functools.partial(pack_kernel, parts=parts, bricks=bricks)...  1.87 us
  transfers between devices with their start and end apart: 1, of which 1 were waited for; matrix products, arithmetic and copies ran while one was open for 0% of the time, Pallas kernels for 14%

profile of v5, /device:TPU:0, one launch (start us, length us, event | category | flops | bytes accessed | tf_op | source)
XLA Modules:
  0.0 55.2 jit_solution(10163388378043176436)
XLA Ops:
  0.0 1.9 %shard_map.82 = bf16[768,128]{1,0:T(8,128)(2,1)} custom-call(s32[2]{0:T(128)} %off_ref.3, bf16[8,8,256]{2,1,0:T(8,128)(2,1)} %stacks_ref.1), custom_call_target="tpu_custom_call" | custom-call | tf_op jit(solution)/shard_map/pallas_call | solution.py:469
  1.9 7.3 %all-to-all-start = ((bf16[32,24,128]{2,1,0:T(8,128)(2,1)}), bf16[32,24,128]{2,1,0:T(8,128)(2,1)S(1)}, u32[]{:S(2)}, u32[]{:S(2)}) async-start(bf16[32,24,128]{2,1,0:T(8,128)(2,1)} %bitcast.8), calls=%async_computation | async-start | bytes 393216 | tf_op jit(solution)/shard_map/all_to_all | solution.py:475
  9.2 7.7 %shard_map.83 = (f32[24,256]{1,0:T(8,128)}, bf16[5,384,256]{2,1,0:T(8,128)(2,1)}, bf16[3,6,128,256]{3,2,1,0:T(8,128)(2,1)}, bf16[3,6,128,256]{3,2,1,0:T(8,128)(2...) custom-call(bf16[4,27,32,32]{3,2,1,0:T(8,128)(2,1)} %refs_0_.1, f32[4,32]{1,0:T(4,128)} %refs_1_.1, ...), custom_call_target="tpu_custom_call" | custom-call | flops 4000000 | bytes 9000000 | tf_op jit(solution)/shard_map/pallas_call | solution.py:484
  16.8 2.0 %all-to-all-done = bf16[32,24,128]{2,1,0:T(8,128)(2,1)S(1)} async-done(((bf16[32,24,128]{2,1,0:T(8,128)(2,1)}), bf16[32,24,128]{2,1,0:T(8,128)(2,1)S(1)}, u32[]{:S(2)}, u32[]{:S(2)}) %all-to-all-start) | async-done | bytes 196640 | tf_op jit(solution)/shard_map/all_to_all | solution.py:475
  18.8 0.0 copy-start
  18.8 0.7 %copy-done = bf16[32,24,128]{2,1,0:T(8,128)(2,1)} copy-done((bf16[32,24,128]{2,1,0:T(8,128)(2,1)}, bf16[32,24,128]{2,1,0:T(8,128)(2,1)S(1)}, u32[]{:S(2)}) %copy-start) | copy-done | bytes 196632
  19.5 23.8 %shard_map.84 = f32[16,8,128]{2,1,0:T(8,128)} custom-call(s32[2]{0:T(128)} %off_ref.3, s32[2]{0:T(128)} %ramp_ref.1, bf16[768,128]{1,0:T(8,128)(2,1)} %bitcast.9, f32[24,256]{1,0:T(8,128)} %get-tuple-element.11.rows_ref, bf16[5,384,256]{2,1,0:T(8,128)(2,1)} %get-tuple-element.12.refs_0_, bf16[3,6,128,256]{3,2,1,0:T(8,128)(2,1)} %get-tuple-element.13.refs_1_, ...), custom_call_target="tpu_custom_call" | custom-call | flops 20000000000 | bytes 9000000 | tf_op jit(solution)/shard_map/pallas_call | solution.py:509
  43.3 10.8 %all_to_all.16 = f32[16,8,128]{2,1,0:T(8,128)S(1)} all-to-all(f32[16,8,128]{2,1,0:T(8,128)} %shard_map.84), channel_id=1, replica_groups=mesh['gz'=4,'gy'=4,'gx'=2] {'gz','gy'}, dimensions={0} | all-to-all | bytes 131072 | tf_op jit(solution)/shard_map/all_to_all | solution.py:520
  54.2 0.2 reshape.6
  54.4 0.8 %copy.11 = f32[8,8,128]{2,1,0:T(8,128)} copy(f32[8,8,128]{1,0,2:T(8,128)S(1)} %reshape.6) | data formatting | bytes 65536 | tf_op jit(solution)/shard_map/reshape | solution.py:522
  (1 shorter events, 0.0 us)
Async XLA Ops:
  1.9 17.0 %all-to-all-start = ((bf16[32,24,128]{2,1,0:T(8,128)(2,1)}), bf16[32,24,128]{2,1,0:T(8,128)(2,1)S(1)}, u32[]{:S(2)}, u32[]{:S(2)}) async-start(bf16[32,24,128]{2,1,0:T(8,128)(2,1)} %bitcast.8), calls=%async_computation | async-start | bytes 393216 | tf_op jit(solution)/shard_map/all_to_all | solution.py:475
  18.8 0.7 %copy-start = (bf16[32,24,128]{2,1,0:T(8,128)(2,1)}, bf16[32,24,128]{2,1,0:T(8,128)(2,1)S(1)}, u32[]{:S(2)}) copy-start(bf16[32,24,128]{2,1,0:T(8,128)(2,1)S(1)} %all-to-all-done) | copy-start | bytes 589828

commit v6 on v5

--- a/solution.py
+++ b/solution.py
@@ -424,10 +424,10 @@
             size = spacing * NY // row_parts
             for y in range(row_parts):
                 for b in range(2):
-                    for x in range(4):
-                        out_ref[
-                            (2 * m + b) * row_parts + y, 2 * x + phase : 2 * x + phase + 1, 0:size
-                        ] = heads[4 * b + x : 4 * b + x + 1, y * size : (y + 1) * size]
+                    lanes = slice(size * phase, size * (phase + 1))
+                    out_ref[(2 * m + b) * row_parts + y, :, lanes] = heads[
+                        4 * b : 4 * b + 4, y * size : (y + 1) * size
+                    ]
 
     fetches[0].wait()
     for k in range(GROUPS[0] // 2):
@@ -508,7 +508,7 @@
     )
     logits = pl.pallas_call(
         conv_kernel,
-        out_shape=jax.ShapeDtypeStruct((parts, SLAB, 128), F32),
+        out_shape=jax.ShapeDtypeStruct((parts, SLAB // 2, 128), F32),
         in_specs=[smem, smem, vmem(), vmem()] + [hbm] * 5,
         out_specs=vmem(),
         scratch_shapes=scratch,
@@ -518,7 +518,7 @@
         ),
     )(offsets, ramp_width, pieces, rows, *weights)
     logits = lax.all_to_all(logits, ("gz", "gy"), 0, 0, tiled=True)
-    logits = logits[:, :, : depth_b * rows_b].transpose(2, 0, 1)
+    logits = logits.reshape(BX, depth_b * rows_b).T
     return logits.reshape(depth_b, rows_b, BX)
 
 

time: 55.5 us -> 55 us (level)
    reshape x2 -> x1, local copies, waits for them, and re-layouts: 1 us -> 0.09 us  [body(): logits = logits.reshape(BX, depth_b * rows_b).T]
    transpose x1, local copies, waits for them, and re-layouts: 0.01 us -> 0.7 us  [body(): logits = logits.reshape(BX, depth_b * rows_b).T]
where the time goes in v6:
time: 55 us; the launch traced here: 54.7 us
  Pallas kernels  33.3 us (61%)
  blocking collectives  10.6 us (19%)
  starting transfers between devices  7.3 us (13%)
  waiting for transfers between devices  1.99 us (4%)
  local copies, waits for them, and re-layouts  1.47 us (3%)
    pallas_call x1, Pallas kernels, body(): pl.pallas_call(conv_kernel, out_shape=jax.ShapeDtypeStruct((parts, SLAB /...  23.8 us
    all_to_all x1, blocking collectives, body(): logits = lax.all_to_all(logits, ('gz', 'gy'), 0, 0, tiled=True)  10.6 us
    pallas_call x1, Pallas kernels, body(): pl.pallas_call(weights_kernel, out_shape=[small] + shapes, in_specs=[hbm]...  7.66 us
    all_to_all x1, starting transfers between devices, body(): pieces = lax.all_to_all(pieces, ('gz', 'gy', 'gx'), 0, 0, tiled=True)  7.3 us
    all_to_all x1, waiting for transfers between devices, body(): pieces = lax.all_to_all(pieces, ('gz', 'gy', 'gx'), 0, 0, tiled=True)  1.99 us
    pallas_call x1, Pallas kernels, body(): pl.pallas_call(functools.partial(pack_kernel, parts=parts, bricks=bricks)...  1.87 us
  transfers between devices with their start and end apart: 1, of which 1 were waited for; matrix products, arithmetic and copies ran while one was open for 0% of the time, Pallas kernels for 14%

profile of v6, /device:TPU:0, one launch (start us, length us, event | category | flops | bytes accessed | tf_op | source)
XLA Modules:
  0.0 54.7 jit_solution(15089459597119992168)
XLA Ops:
  0.0 1.9 %shard_map.82 = bf16[768,128]{1,0:T(8,128)(2,1)} custom-call(s32[2]{0:T(128)} %off_ref.3, bf16[8,8,256]{2,1,0:T(8,128)(2,1)} %stacks_ref.1), custom_call_target="tpu_custom_call" | custom-call | tf_op jit(solution)/shard_map/pallas_call | solution.py:469
  1.9 7.3 %all-to-all-start = ((bf16[32,24,128]{2,1,0:T(8,128)(2,1)}), bf16[32,24,128]{2,1,0:T(8,128)(2,1)S(1)}, u32[]{:S(2)}, u32[]{:S(2)}) async-start(bf16[32,24,128]{2,1,0:T(8,128)(2,1)} %bitcast.6), calls=%async_computation | async-start | bytes 393216 | tf_op jit(solution)/shard_map/all_to_all | solution.py:475
  9.2 7.7 %shard_map.83 = (f32[24,256]{1,0:T(8,128)}, bf16[5,384,256]{2,1,0:T(8,128)(2,1)}, bf16[3,6,128,256]{3,2,1,0:T(8,128)(2,1)}, bf16[3,6,128,256]{3,2,1,0:T(8,128)(2...) custom-call(bf16[4,27,32,32]{3,2,1,0:T(8,128)(2,1)} %refs_0_.1, f32[4,32]{1,0:T(4,128)} %refs_1_.1, ...), custom_call_target="tpu_custom_call" | custom-call | flops 4000000 | bytes 9000000 | tf_op jit(solution)/shard_map/pallas_call | solution.py:484
  16.8 2.0 %all-to-all-done = bf16[32,24,128]{2,1,0:T(8,128)(2,1)S(1)} async-done(((bf16[32,24,128]{2,1,0:T(8,128)(2,1)}), bf16[32,24,128]{2,1,0:T(8,128)(2,1)S(1)}, u32[]{:S(2)}, u32[]{:S(2)}) %all-to-all-start) | async-done | bytes 196640 | tf_op jit(solution)/shard_map/all_to_all | solution.py:475
  18.8 0.0 copy-start
  18.8 0.7 %copy-done = bf16[32,24,128]{2,1,0:T(8,128)(2,1)} copy-done((bf16[32,24,128]{2,1,0:T(8,128)(2,1)}, bf16[32,24,128]{2,1,0:T(8,128)(2,1)S(1)}, u32[]{:S(2)}) %copy-start) | copy-done | bytes 196632
  19.5 23.8 %shard_map.84 = f32[16,4,128]{2,1,0:T(4,128)} custom-call(s32[2]{0:T(128)} %off_ref.3, s32[2]{0:T(128)} %ramp_ref.1, bf16[768,128]{1,0:T(8,128)(2,1)} %bitcast.8, f32[24,256]{1,0:T(8,128)} %get-tuple-element.11.rows_ref, bf16[5,384,256]{2,1,0:T(8,128)(2,1)} %get-tuple-element.12.refs_0_, bf16[3,6,128,256]{3,2,1,0:T(8,128)(2,1)} %get-tuple-element.13.refs_1_, ...), custom_call_target="tpu_custom_call" | custom-call | flops 20000000000 | bytes 9000000 | tf_op jit(solution)/shard_map/pallas_call | solution.py:509
  43.3 10.6 %all_to_all.16 = f32[16,4,128]{2,1,0:T(4,128)S(1)} all-to-all(f32[16,4,128]{2,1,0:T(4,128)} %shard_map.84), channel_id=1, replica_groups=mesh['gz'=4,'gy'=4,'gx'=2] {'gz','gy'}, dimensions={0} | all-to-all | bytes 65536 | tf_op jit(solution)/shard_map/all_to_all | solution.py:520
  53.9 0.1 reshape.8
  54.0 0.7 %copy.11 = f32[64,128]{1,0:T(8,128)} copy(f32[64,128]{0,1:T(8,128)S(1)} %bitcast.7) | data formatting | bytes 65536 | tf_op jit(solution)/shard_map/transpose | solution.py:521
Async XLA Ops:
  1.9 17.0 %all-to-all-start = ((bf16[32,24,128]{2,1,0:T(8,128)(2,1)}), bf16[32,24,128]{2,1,0:T(8,128)(2,1)S(1)}, u32[]{:S(2)}, u32[]{:S(2)}) async-start(bf16[32,24,128]{2,1,0:T(8,128)(2,1)} %bitcast.6), calls=%async_computation | async-start | bytes 393216 | tf_op jit(solution)/shard_map/all_to_all | solution.py:475
  18.8 0.7 %copy-start = (bf16[32,24,128]{2,1,0:T(8,128)(2,1)}, bf16[32,24,128]{2,1,0:T(8,128)(2,1)S(1)}, u32[]{:S(2)}) copy-start(bf16[32,24,128]{2,1,0:T(8,128)(2,1)S(1)} %all-to-all-done) | copy-start | bytes 589828
